TPU v7x, 32 devices: a whole 2x2x4 slice. The times are simulated.
32 devices in a mesh: space: 16 (over z, y, x), blk: 2 (over core).
Axes of the slice: x: 2, y: 2, z: 4, core: 2. Of those that a mesh axis runs over, the one named last changes fastest.
Arguments:
- coords: float32 [32, 2, 256], P(('space', 'blk'))
- values: float32 [32, 32, 256], P(('space', 'blk')), may hold values from -6 to 6
- valid: int32 [32], P(('space', 'blk')), may hold values from 128 to 256, as said below
- neighbours: int32 [32, 3], P(('space', 'blk')), may hold values from -1 to 30, as said below
- grid: float32 [32, 2, 256], P(('space', 'blk'))
- sources: int32 [32, 3], P(('space', 'blk')), may hold values from -1 to 31, as said below
- theta: float32 [6], replicated, may hold values from 0.05 to 1.6
Outputs:
- whitened: float32 [32, 32, 256], P(('space', 'blk'))
- predicted: float32 [32, 32, 256], P(('space', 'blk'))
- loglik: float32 [], replicated
Inputs may be any that keep to these rules, and one draw needn't show every extreme that they name: `neighbours`: a row lists distinct earlier blocks b - o with 1 <= o <= 4, always including b - 1, entries below 0 given as -1. `sources`: tile t lists distinct blocks e - o with 0 <= o < 4, always including e, e the last block of the device holding tile t, entries below 0 given as -1. `valid`: every even-numbered block is full.
All inputs are finite; a program needn't handle non-finite values.
Results may differ from a plain program's by a relative error of at most 0.0003.
Values sent between devices are 32-bit elements; how exact they have to be, the bound alone decides.
No kernel may reach another device: no remote copies, remote signals or barrier semaphores. Data moves between devices by JAX's collectives and lax.ppermute only.
A program may use at most 128 MiB of HBM per device.

v0:
```python
import math

import jax
import jax.numpy as jnp
from jax import lax
from jax.sharding import PartitionSpec as P

K = 3
HIST = 2
NEWTON = 8


def passed_along(value, axis, steps):
    count = lax.axis_size(axis)
    initial, last = (max(0, -steps), min(count, count - steps))
    return lax.ppermute(value, axis, [(source, source + steps) for source in range(initial, last)])


def lower_solve(factor, rhs):
    return lax.linalg.triangular_solve(factor, rhs, left_side=True, lower=True)


def site_mask(valid_rows, width):
    return (jnp.arange(width)[None, :] < valid_rows[:, None]).astype(jnp.float32)


def tukey_inverse(data, theta):
    shape_g = theta[3]
    shape_h = theta[4]
    omega = theta[5]
    target = data / omega
    point = jnp.zeros_like(target)
    for step in range(NEWTON):
        grow = jnp.exp(shape_g * point)
        heavy = jnp.exp(0.5 * shape_h * point * point)
        value = (grow - 1.0) / shape_g * heavy
        slope = grow * heavy + shape_h * point * value
        point = point - (value - target) / slope
    grow = jnp.exp(shape_g * point)
    heavy = jnp.exp(0.5 * shape_h * point * point)
    value = (grow - 1.0) / shape_g * heavy
    slope = grow * heavy + shape_h * point * value
    return (point, jnp.log(omega * slope))


def tukey_forward(point, theta):
    return (
        theta[5]
        * (jnp.exp(theta[3] * point) - 1.0)
        / theta[3]
        * jnp.exp(0.5 * theta[4] * point * point)
    )


def covariance(first, second, theta):
    across = first[0][:, None] - second[0][None, :]
    along = first[1][:, None] - second[1][None, :]
    return theta[0] * jnp.exp(-jnp.sqrt(across * across + along * along) / theta[1])


def factor_of(points, weight, theta):
    matrix = covariance(points, points, theta) * weight[:, None] * weight[None, :]
    matrix = matrix + jnp.diag(theta[2] * weight + 1.0 - weight)
    return jnp.linalg.cholesky(matrix)


def fetch(window, ids, base, reps, theta):
    present = (ids >= 0).astype(jnp.float32)
    local = jnp.where(ids >= 0, ids - base, 0)
    rows = jnp.take(window, local, axis=0)
    points = rows[:, 0:2, :].transpose(1, 0, 2).reshape(2, -1)
    data = rows[:, 2 : 2 + reps, :]
    data = tukey_inverse(data, theta)[0]
    weight = (rows[:, 2 + reps, :] * present[:, None]).reshape(-1)
    data = data.transpose(1, 0, 2).reshape(reps, -1) * weight[None, :]
    return (points, weight, data)


def body(coords, values, valid, neighbours, grid, sources, theta):
    blocks = coords.shape[0]
    width = coords.shape[2]
    reps = values.shape[1]
    tiles = grid.shape[0]
    n_blocks_axis = lax.axis_size("blk")
    group = blocks * n_blocks_axis
    space_index = lax.axis_index("space")
    first_id = (space_index * n_blocks_axis + lax.axis_index("blk")) * blocks
    base = (space_index - HIST) * group
    masks = site_mask(valid, width)
    latent, logjac = tukey_inverse(values, theta)
    packed = jnp.concatenate([coords, values, masks[:, None, :]], axis=1)
    grouped = lax.all_gather(packed, "blk", axis=0, tiled=True)
    pieces = [grouped]
    for step in range(1, HIST + 1):
        pieces.insert(0, passed_along(grouped, "space", step))
    window = jnp.concatenate(pieces, axis=0)

    def condition(index):
        ids = jnp.concatenate([neighbours[index], (first_id + index)[None]])
        points, weight, data = fetch(window, ids, base, reps, theta)
        factor = factor_of(points, weight, theta)
        white = lower_solve(factor, data.T)
        own_white = white[K * width :, :].T
        logdiag = jnp.log(jnp.diagonal(factor))[K * width :]
        term = -0.5 * jnp.sum(own_white * own_white) - reps * jnp.sum(logdiag)
        term = term - 0.5 * reps * math.log(2.0 * math.pi) * jnp.sum(masks[index])
        term = term - jnp.sum(logjac[index] * masks[index][None, :])
        return (own_white, term)

    whitened, terms = lax.map(condition, jnp.arange(blocks, dtype=jnp.int32))

    def predict(index):
        points, weight, data = fetch(window, sources[index], base, reps, theta)
        factor = factor_of(points, weight, theta)
        solved = lower_solve(factor, data.T)
        cross = covariance(points, grid[index], theta) * weight[:, None]
        reach = lower_solve(factor, cross)
        mean = jnp.dot(
            solved.T, reach, precision=lax.Precision.HIGHEST, preferred_element_type=jnp.float32
        )
        return tukey_forward(mean, theta)

    predicted = lax.map(predict, jnp.arange(tiles, dtype=jnp.int32))
    total, count = lax.psum((jnp.sum(terms), jnp.sum(valid.astype(jnp.float32))), ("space", "blk"))
    loglik = total / (reps * count)
    return (whitened, predicted, loglik)


def solution(mesh):
    return jax.shard_map(
        body,
        mesh=mesh,
        in_specs=(
            P(("space", "blk"), None, None),
            P(("space", "blk"), None, None),
            P(("space", "blk")),
            P(("space", "blk"), None),
            P(("space", "blk"), None, None),
            P(("space", "blk"), None),
            P(),
        ),
        out_specs=(P(("space", "blk"), None, None), P(("space", "blk"), None, None), P()),
        check_vma=False,
    )
```

profile of v0, /device:TPU:0, one launch (start us, length us, event | category | flops | bytes accessed | tf_op | source)
XLA Modules:
  0.0 685.8 jit_solution(17383669891223954250)
XLA Ops:
  39.5 11.7 %cholesky.309 = f32[128,128]{1,0:T(8,128)S(1)} custom-call(f32[128,128]{1,0:T(8,128)S(1)} %cholesky.809), custom_call_target="Cholesky" | custom-call | tf_op jit(solution)/shard_map/while/body/eval_jaxpr/jit(cholesky)/cholesky | solution.py:64
  64.3 11.7 %cholesky.721 = f32[128,128]{1,0:T(8,128)S(1)} custom-call(f32[128,128]{1,0:T(8,128)S(1)} %cholesky.842), custom_call_target="Cholesky" | custom-call | tf_op jit(solution)/shard_map/while/body/eval_jaxpr/jit(cholesky)/cholesky | solution.py:64
  76.8 9.8 %custom-call.93 = f32[1,128,128]{1,2,0:T(8,128)S(1)} custom-call(f32[1,128,128]{2,1,0:T(8,128)S(1)} %get-tuple-element.152), custom_call_target="InvertDiagBlocksLowerTriangular" | custom-call | tf_op jit(solution)/shard_map/while/body/eval_jaxpr/jit(cholesky)/cholesky | solution.py:64
  90.5 11.9 %cholesky.332 = f32[128,128]{1,0:T(8,128)S(1)} custom-call(f32[128,128]{1,0:T(8,128)S(1)} %cholesky.813), custom_call_target="Cholesky" | custom-call | tf_op jit(solution)/shard_map/while/body/eval_jaxpr/jit(cholesky)/cholesky | solution.py:64
  103.1 9.8 %custom-call.94 = f32[1,128,128]{1,2,0:T(8,128)S(1)} custom-call(f32[1,128,128]{2,1,0:T(8,128)S(1)} %get-tuple-element.149), custom_call_target="InvertDiagBlocksLowerTriangular" | custom-call | tf_op jit(solution)/shard_map/while/body/eval_jaxpr/jit(cholesky)/cholesky | solution.py:64
  116.2 11.7 %cholesky.357 = f32[128,128]{1,0:T(8,128)S(1)} custom-call(f32[128,128]{1,0:T(8,128)S(1)} %cholesky.818), custom_call_target="Cholesky" | custom-call | tf_op jit(solution)/shard_map/while/body/eval_jaxpr/jit(cholesky)/cholesky | solution.py:64
  128.6 9.8 %custom-call.104 = f32[1,128,128]{1,2,0:T(8,128)S(1)} custom-call(f32[1,128,128]{2,1,0:T(8,128)S(1)} %get-tuple-element.146), custom_call_target="InvertDiagBlocksLowerTriangular" | custom-call | tf_op jit(solution)/shard_map/while/body/eval_jaxpr/jit(cholesky)/cholesky/custom-call.16 | solution.py:64
  142.2 11.7 %cholesky.376 = f32[128,128]{1,0:T(8,128)S(1)} custom-call(f32[128,128]{1,0:T(8,128)S(1)} %cholesky.823), custom_call_target="Cholesky" | custom-call | tf_op jit(solution)/shard_map/while/body/eval_jaxpr/jit(cholesky)/cholesky | solution.py:64
  154.5 9.8 %custom-call.105 = f32[1,128,128]{1,2,0:T(8,128)S(1)} custom-call(f32[1,128,128]{2,1,0:T(8,128)S(1)} %get-tuple-element.143), custom_call_target="InvertDiagBlocksLowerTriangular" | custom-call | tf_op jit(solution)/shard_map/while/body/eval_jaxpr/jit(cholesky)/cholesky/custom-call.17 | solution.py:64
  167.8 12.2 %cholesky.662 = f32[128,128]{1,0:T(8,128)S(1)} custom-call(f32[128,128]{1,0:T(8,128)S(1)} %cholesky.828), custom_call_target="Cholesky" | custom-call | tf_op jit(solution)/shard_map/while/body/eval_jaxpr/jit(cholesky)/cholesky | solution.py:64
  180.6 9.8 %custom-call.106 = f32[1,128,128]{1,2,0:T(8,128)S(1)} custom-call(f32[1,128,128]{2,1,0:T(8,128)S(1)} %get-tuple-element.140), custom_call_target="InvertDiagBlocksLowerTriangular" | custom-call | tf_op jit(solution)/shard_map/while/body/eval_jaxpr/jit(cholesky)/cholesky/custom-call.18 | solution.py:64
  193.8 11.7 %cholesky.678 = f32[128,128]{1,0:T(8,128)S(1)} custom-call(f32[128,128]{1,0:T(8,128)S(1)} %cholesky.833), custom_call_target="Cholesky" | custom-call | tf_op jit(solution)/shard_map/while/body/eval_jaxpr/jit(cholesky)/cholesky | solution.py:64
  206.1 9.8 %custom-call.107 = f32[1,128,128]{1,2,0:T(8,128)S(1)} custom-call(f32[1,128,128]{2,1,0:T(8,128)S(1)} %get-tuple-element.137), custom_call_target="InvertDiagBlocksLowerTriangular" | custom-call | tf_op jit(solution)/shard_map/while/body/eval_jaxpr/jit(cholesky)/cholesky/custom-call.19 | solution.py:64
  218.9 11.9 %cholesky.694 = f32[128,128]{1,0:T(8,128)S(1)} custom-call(f32[128,128]{1,0:T(8,128)S(1)} %cholesky.838), custom_call_target="Cholesky" | custom-call | tf_op jit(solution)/shard_map/while/body/eval_jaxpr/jit(cholesky)/cholesky | solution.py:64
  231.4 9.8 %custom-call.108 = f32[1,128,128]{1,2,0:T(8,128)S(1)} custom-call(f32[1,128,128]{2,1,0:T(8,128)S(1)} %get-tuple-element.134), custom_call_target="InvertDiagBlocksLowerTriangular" | custom-call | tf_op jit(solution)/shard_map/while/body/eval_jaxpr/jit(cholesky)/cholesky/custom-call.20 | solution.py:64
  243.9 11.7 %cholesky.708 = f32[128,128]{1,0:T(8,128)S(1)} custom-call(f32[128,128]{1,0:T(8,128)S(1)} %convolution_subtract_fusion.16), custom_call_target="Cholesky" | custom-call | tf_op jit(solution)/shard_map/while/body/eval_jaxpr/jit(cholesky)/cholesky | solution.py:64
  273.2 28.0 %while.2 = (s32[]{:T(128)}, f32[1024,1024]{1,0:T(8,128)}, s32[8,2]{0,1:T(2,128)S(1)}, f32[8,128,128]{2,1,0:T(8,128)}, s32[]{:T(128)}) while((s32[]{:T(128)}, f32[1024,1024]{1,0:T(8,128)}, s32[8,2]{0,1:T(2,128)S(1)}, f32[8,128,128]{2,1,0:T(8,128)}, s32[]{:T(128)}) %tuple.119), condition=%wide.while_cond, body=%wide.while_body.sunk | while | flops 2 | bytes 132205 | solution.py:20
  301.2 79.8 %custom-call.95 = f32[8,128,128]{1,2,0:T(8,128)S(1)} custom-call(f32[8,128,128]{2,1,0:T(8,128)} %get-tuple-element.59), custom_call_target="InvertDiagBlocksLowerTriangular" | custom-call | tf_op jit(solution)/shard_map/while/body/eval_jaxpr/triangular_solve | solution.py:20
  393.0 9.8 %custom-call.109 = f32[1,128,128]{1,2,0:T(8,128)S(1)} custom-call(f32[1,128,128]{2,1,0:T(8,128)S(1)} %get-tuple-element.130), custom_call_target="InvertDiagBlocksLowerTriangular" | custom-call | tf_op jit(solution)/shard_map/while/body/eval_jaxpr/jit(cholesky)/cholesky/custom-call.16 | solution.py:64
  405.6 11.7 %cholesky.732 = f32[128,128]{1,0:T(8,128)S(1)} custom-call(f32[128,128]{1,0:T(8,128)S(1)} %cholesky.846), custom_call_target="Cholesky" | custom-call | tf_op jit(solution)/shard_map/while/body/eval_jaxpr/jit(cholesky)/cholesky | solution.py:64
  417.4 9.8 %custom-call.110 = f32[1,128,128]{1,2,0:T(8,128)S(1)} custom-call(f32[1,128,128]{2,1,0:T(8,128)S(1)} %get-tuple-element.127), custom_call_target="InvertDiagBlocksLowerTriangular" | custom-call | tf_op jit(solution)/shard_map/while/body/eval_jaxpr/jit(cholesky)/cholesky/custom-call.17 | solution.py:64
  429.3 11.7 %cholesky.749 = f32[128,128]{1,0:T(8,128)S(1)} custom-call(f32[128,128]{1,0:T(8,128)S(1)} %cholesky.851), custom_call_target="Cholesky" | custom-call | tf_op jit(solution)/shard_map/while/body/eval_jaxpr/jit(cholesky)/cholesky | solution.py:64
  441.1 9.8 %custom-call.111 = f32[1,128,128]{1,2,0:T(8,128)S(1)} custom-call(f32[1,128,128]{2,1,0:T(8,128)S(1)} %get-tuple-element.124), custom_call_target="InvertDiagBlocksLowerTriangular" | custom-call | tf_op jit(solution)/shard_map/while/body/eval_jaxpr/jit(cholesky)/cholesky/custom-call.18 | solution.py:64
  452.8 11.7 %cholesky.764 = f32[128,128]{1,0:T(8,128)S(1)} custom-call(f32[128,128]{1,0:T(8,128)S(1)} %cholesky.856), custom_call_target="Cholesky" | custom-call | tf_op jit(solution)/shard_map/while/body/eval_jaxpr/jit(cholesky)/cholesky | solution.py:64
  464.5 10.0 %custom-call.112 = f32[1,128,128]{1,2,0:T(8,128)S(1)} custom-call(f32[1,128,128]{2,1,0:T(8,128)S(1)} %get-tuple-element.121), custom_call_target="InvertDiagBlocksLowerTriangular" | custom-call | tf_op jit(solution)/shard_map/while/body/eval_jaxpr/jit(cholesky)/cholesky/custom-call.19 | solution.py:64
  476.3 11.7 %cholesky.779 = f32[128,128]{1,0:T(8,128)S(1)} custom-call(f32[128,128]{1,0:T(8,128)S(1)} %cholesky.861), custom_call_target="Cholesky" | custom-call | tf_op jit(solution)/shard_map/while/body/eval_jaxpr/jit(cholesky)/cholesky | solution.py:64
  488.1 9.8 %custom-call.113 = f32[1,128,128]{1,2,0:T(8,128)S(1)} custom-call(f32[1,128,128]{2,1,0:T(8,128)S(1)} %get-tuple-element.118), custom_call_target="InvertDiagBlocksLowerTriangular" | custom-call | tf_op jit(solution)/shard_map/while/body/eval_jaxpr/jit(cholesky)/cholesky/custom-call.20 | solution.py:64
  499.4 11.7 %cholesky.793 = f32[128,128]{1,0:T(8,128)S(1)} custom-call(f32[128,128]{1,0:T(8,128)S(1)} %convolution_subtract_fusion.15), custom_call_target="Cholesky" | custom-call | tf_op jit(solution)/shard_map/while/body/eval_jaxpr/jit(cholesky)/cholesky | solution.py:64
  520.6 21.7 %while.3 = (s32[]{:T(128)}, f32[768,768]{1,0:T(8,128)}, s32[6,2]{0,1:T(2,128)S(1)}, f32[6,128,128]{2,1,0:T(8,128)}, s32[]{:T(128)}) while((s32[]{:T(128)}, f32[768,768]{1,0:T(8,128)}, s32[6,2]{0,1:T(2,128)S(1)}, f32[6,128,128]{2,1,0:T(8,128)}, s32[]{:T(128)}) %tuple.122), condition=%wide.while_cond.1, body=%wide.while_body.1.sunk | while | flops 2 | bytes 132205 | solution.py:20
  542.3 59.8 %custom-call.96 = f32[6,128,128]{1,2,0:T(8,128)S(1)} custom-call(f32[6,128,128]{2,1,0:T(8,128)} %get-tuple-element.74), custom_call_target="InvertDiagBlocksLowerTriangular" | custom-call | tf_op jit(solution)/shard_map/while/body/eval_jaxpr/triangular_solve | solution.py:20
  619.0 17.3 %gather_fusion.2 = f32[1024]{0:T(1024)S(1)} fusion(f32[1024,1024]{1,0:T(8,128)} %get-tuple-element.98, s32[1024]{0:T(1024)S(1)} %bitcast.296), kind=kCustom, calls=%fused_computation.2 | custom fusion | bytes 16384 | tf_op jit(solution)/shard_map/while/body/eval_jaxpr/jit(diagonal)/cond/branch_0_fun/gather | solution.py:104
  638.8 41.3 %all-reduce.2 = (f32[]{:T(128)}, f32[]{:T(128)}) all-reduce(f32[]{:T(128)S(6)} %sub.592, f32[]{:T(128)} %bitcast.80), channel_id=1, replica_groups=mesh['space'=16,'blk'=2] {'space','blk'}, use_global_device_ids=true, to_apply=%region_32.38 | all-reduce | flops 2 | bytes 16 | tf_op jit(solution)/shard_map/psum | solution.py:124
  (222 shorter events, 185.9 us)
Async XLA Ops:
  4.0 22.8 %collective-permute-start = (f32[2,35,256]{2,1,0:T(8,128)S(1)}, f32[2,35,256]{2,1,0:T(8,128)S(1)}, u32[]{:S(2)}, u32[]{:S(2)}) collective-permute-start(f32[2,35,256]{2,1,0:T(8,128)S(1)} %all_gather.3), channel_id=1, source_target_pairs={{0,4},{2,6},{4,8},{6,10},{8,12},{10,14},{12,16},{14,18},{16,20},{1... | collective-permute-start | bytes 215048 | tf_op jit(solution)/shard_map/ppermute | solution.py:16
  8.8 18.0 %collective-permute-start.1 = (f32[2,35,256]{2,1,0:T(8,128)S(1)}, f32[2,35,256]{2,1,0:T(8,128)S(1)}, u32[]{:S(2)}, u32[]{:S(2)}) collective-permute-start(f32[2,35,256]{2,1,0:T(8,128)S(1)} %all_gather.3), channel_id=1, source_target_pairs={{0,2},{2,4},{4,6},{6,8},{8,10},{10,12},{12,14},{14,16},{16,18},{18... | collective-permute-start | bytes 215048 | tf_op jit(solution)/shard_map/ppermute | solution.py:16
  37.5 1.9 copy-start
  62.9 1.4 copy-start.1
  273.2 119.8 %copy-start.2 = (f32[3,4,8,256]{3,2,1,0:T(8,128)S(1)}, f32[3,4,8,256]{3,2,1,0:T(8,128)}, u32[]{:S(2)}) copy-start(f32[3,4,8,256]{3,2,1,0:T(8,128)} %subtract_bitcast_fusion.1) | copy-start | bytes 294916
  404.2 107.0 %copy-start.5 = (f32[128]{0:T(128)S(1)}, f32[128]{0:T(128)}, u32[]{:S(2)}) copy-start(f32[128]{0:T(128)} %get-tuple-element.129) | copy-start | bytes 1540
  451.2 69.4 %copy-start.6 = (s32[6]{0:T(128)S(1)}, s32[6]{0:T(128)}, u32[]{:S(2)}) copy-start(s32[6]{0:T(128)} %iota_multiply_fusion) | copy-start | bytes 76
  497.9 111.3 %copy-start.3 = (f32[1,1,256]{2,1,0:T(1,128)S(1)}, f32[1,1,256]{2,1,0:T(1,128)}, u32[]{:S(2)}) copy-start(f32[1,1,256]{2,1,0:T(1,128)} %get-tuple-element.182) | copy-start | bytes 3076
  497.9 111.3 %copy-start.4 = (f32[1,1,256]{2,1,0:T(1,128)S(1)}, f32[1,1,256]{2,1,0:T(1,128)}, u32[]{:S(2)}) copy-start(f32[1,1,256]{2,1,0:T(1,128)} %get-tuple-element.183) | copy-start | bytes 3076
where the time goes:
time: 697 us; the launch traced here: 686 us
  other arithmetic  476 us (68%)
  local copies, waits for them, and re-layouts  77.4 us (11%)
  matrix products  61.6 us (9%)
  blocking collectives  43.2 us (6%)
  between operations  19.1 us (3%)
  starting transfers between devices  8.16 us (1%)
    another operation x54, other arithmetic, factor_of(): return jnp.linalg.cholesky(matrix)  297 us
    another operation x6, other arithmetic, lower_solve(): return lax.linalg.triangular_solve(factor, rhs, left_side=True, lower=True)  148 us
    another operation x42, local copies, waits for them, and re-layouts  49.6 us
    psum x1, blocking collectives, body(): lax.psum((jnp.sum(terms), jnp.sum(valid.astype(jnp.float32))), ('space',...  41.3 us
    another operation x24, matrix products, factor_of(): return jnp.linalg.cholesky(matrix)  33.3 us
    another operation x37, matrix products, lower_solve(): return lax.linalg.triangular_solve(factor, rhs, left_side=True, lower=True)  26 us
    gather x1, local copies, waits for them, and re-layouts, condition(): logdiag = jnp.log(jnp.diagonal(factor))[K * width:]  17.3 us
  transfers between devices with their start and end apart: 2, of which 0 were waited for; matrix products, arithmetic and copies ran while one was open for 2% of the time, Pallas kernels for 0%

commit v1 on v0

v1 whole, which is shorter than its diff:
```python
import functools
import math

import jax
import jax.numpy as jnp
from jax import lax
from jax.experimental import pallas as pl
from jax.experimental.pallas import tpu as pltpu
from jax.sharding import PartitionSpec as P

HIST = 2
NEWTON = 8
TILE = 128
GROUP = (8, 128)
ROWS = 40
HI = lax.Precision.HIGHEST


def passed_along(value, axis, steps):
    count = lax.axis_size(axis)
    initial, last = (max(0, -steps), min(count, count - steps))
    return lax.ppermute(value, axis, [(source, source + steps) for source in range(initial, last)])


def summed_over(value, axis):
    count = lax.axis_size(axis)
    if count & (count - 1):
        total = value
        for _ in range(count - 1):
            value = lax.ppermute(value, axis, [(i, (i + 1) % count) for i in range(count)])
            total = total + value
        return total
    step = 1
    while step < count:
        value = value + lax.ppermute(value, axis, [(i, i ^ step) for i in range(count)])
        step *= 2
    return value


def prepare_kernel(values_ref, coords_ref, valid_ref, theta_ref, packed_ref, extra_ref):
    reps, width = values_ref.shape[1], values_ref.shape[2]
    shape_g, shape_h, omega = theta_ref[3], theta_ref[4], theta_ref[5]
    one = jnp.ones((1, width), jnp.float32)
    inv_g = 1.0 / (one * shape_g)
    inv_omega = 1.0 / (one * omega)
    half_h = 0.5 * shape_h

    def parts(point):
        grow = jnp.exp(shape_g * point)
        heavy = jnp.exp(half_h * point * point)
        value = (grow - 1.0) * inv_g * heavy
        return value, grow * heavy + shape_h * point * value

    for index in range(values_ref.shape[0]):
        lane = lax.broadcasted_iota(jnp.int32, (1, width), 1)
        mask = (lane < valid_ref[index]).astype(jnp.float32)
        target = values_ref[index] * inv_omega
        point = jnp.zeros_like(target)
        for _ in range(NEWTON):
            value, slope = parts(point)
            point = point - (value - target) / slope
        _, slope = parts(point)
        logjac = jnp.log(omega * slope) * mask
        packed_ref[index, 0:reps, :] = point * mask
        packed_ref[index, reps : reps + 2, :] = coords_ref[index]
        packed_ref[index, reps + 2 : reps + 3, :] = mask
        packed_ref[index, reps + 3 :, :] = jnp.zeros((ROWS - reps - 3, width), jnp.float32)
        live = jnp.sum(mask)
        part = -jnp.sum(logjac) - 0.5 * reps * math.log(2.0 * math.pi) * live
        at = lax.broadcasted_iota(jnp.int32, GROUP, 1)
        extra_ref[index] = jnp.where(at == 0, part, jnp.where(at == 1, live, 0.0))


def over_sublanes(x, j):
    return jnp.broadcast_to(x[j : j + 1, :], GROUP)


def over_lanes(x, j):
    return jnp.broadcast_to(x[:, j : j + 1], GROUP)


def factor_tile(rows):
    count = len(rows)
    rows = list(rows)
    sub = lax.broadcasted_iota(jnp.int32, GROUP, 0)
    lane = lax.broadcasted_iota(jnp.int32, GROUP, 1)
    inverse = [jnp.where(lane == sub + 8 * q, 1.0, 0.0).astype(jnp.float32) for q in range(count)]
    pivots = []
    diag = [over_lanes(rows[0], j) for j in range(8)]
    for p in range(count):
        cols = {q: [over_lanes(rows[q], 8 * p + j) for j in range(8)] for q in range(p + 1, count)}
        if p + 1 < count:
            ahead = [over_lanes(rows[p + 1], 8 * (p + 1) + j) for j in range(8)]
        recips, upper, own_rows, own_inv = [], {}, [], []
        pivot = jnp.zeros(GROUP, jnp.float32)
        row, inv = rows[p], inverse[p]
        for j in range(8):
            d = over_sublanes(diag[j], j)
            r = 1.0 / d
            recips.append(r)
            pivot = jnp.where(sub == j, d, pivot)
            for k in range(j + 1, 8):
                upper[j, k] = over_sublanes(diag[k], j)
                diag[k] = diag[k] - (diag[j] * upper[j, k]) * r
            own_rows.append(over_sublanes(row, j))
            own_inv.append(over_sublanes(inv, j))
            if j < 7:
                m = jnp.where(sub > j, diag[j] * r, 0.0)
                row = row - m * own_rows[j]
                inv = inv - m * own_inv[j]
        inverse[p] = inv
        pivots.append(pivot)
        for q in range(p + 1, count):
            t, e = rows[q], inverse[q]
            for j in range(8):
                v = cols[q][j]
                f = v * recips[j]
                if q == p + 1:
                    for k in range(8):
                        ahead[k] = ahead[k] - f * over_sublanes(v, k)
                for k in range(j + 1, 8):
                    cols[q][k] = cols[q][k] - f * upper[j, k]
                t = t - f * own_rows[j]
                e = e - f * own_inv[j]
            rows[q], inverse[q] = t, e
        if p + 1 < count:
            diag = ahead
    return [inverse[q] * lax.rsqrt(pivots[q]) for q in range(count)], pivots


def load_set(blocks, window_ref, theta_ref, reps, width, w_ref, xb_ref, yb_ref, mb_ref, data_at):
    s2, rho, nug = theta_ref[0], theta_ref[1], theta_ref[2]
    slope = -1.0 / jnp.full((1, TILE), rho, jnp.float32)
    per = width // TILE
    for n, (index, present) in enumerate(blocks):
        block = window_ref[index]
        full = jnp.concatenate([block, jnp.zeros((TILE - ROWS, width), jnp.float32)], axis=0)
        turned = jnp.transpose(full)
        at = slice(n * width, (n + 1) * width)
        xb_ref[at, :] = jnp.broadcast_to(turned[:, reps : reps + 1], (width, TILE))
        yb_ref[at, :] = jnp.broadcast_to(turned[:, reps + 1 : reps + 2], (width, TILE))
        mb_ref[at, :] = jnp.broadcast_to(turned[:, reps + 2 : reps + 3] * present, (width, TILE))
        w_ref[at, data_at : data_at + TILE] = turned * present
    sub = lax.broadcasted_iota(jnp.int32, (TILE, TILE), 0)
    lane = lax.broadcasted_iota(jnp.int32, (TILE, TILE), 1)
    for n, (index, present) in enumerate(blocks):
        for part in range(per):
            c = n * per + part
            lanes = slice(part * TILE, (part + 1) * TILE)
            xr = window_ref[index, reps : reps + 1, lanes]
            yr = window_ref[index, reps + 1 : reps + 2, lanes]
            mr = window_ref[index, reps + 2 : reps + 3, lanes] * present

            def tile(at):
                dx = xb_ref[at, :] - xr
                dy = yb_ref[at, :] - yr
                return jnp.exp(jnp.sqrt(dx * dx + dy * dy) * slope) * (mb_ref[at, :] * (mr * s2))

            for r in range(c):
                at = slice(r * TILE, (r + 1) * TILE)
                w_ref[at, c * TILE : (c + 1) * TILE] = tile(at)
            at = slice(c * TILE, (c + 1) * TILE)
            w_ref[at, at] = jnp.where(sub == lane, mr * (s2 + nug) + (1.0 - mr), tile(at))


def eliminate(count, total, w_ref, li_ref, ld_ref):
    def step(k, carry):
        off = pl.multiple_of(k * TILE, TILE)
        rows = [w_ref[pl.ds(off + 8 * q, 8), pl.ds(off, TILE)] for q in range(TILE // 8)]
        inverse, pivots = factor_tile(rows)
        logs = jnp.zeros(GROUP, jnp.float32)
        for q in range(TILE // 8):
            li_ref[8 * q : 8 * q + 8, :] = inverse[q]
            logs = logs + jnp.log(pivots[q])
        ld_ref[k] = logs
        for kk in range(count):

            @pl.when(k == kk)
            def _():
                at = slice(kk * TILE, (kk + 1) * TILE)
                start = (kk + 1) * TILE
                w_ref[at, start:total] = lax.dot(
                    li_ref[...], w_ref[at, start:total], precision=HI, preferred_element_type=jnp.float32
                )
                for i in range(kk + 1, count):
                    rows_at = slice(i * TILE, (i + 1) * TILE)
                    w_ref[rows_at, i * TILE : total] -= lax.dot_general(
                        w_ref[at, rows_at],
                        w_ref[at, i * TILE : total],
                        (((0,), (0,)), ((), ())),
                        precision=HI,
                        preferred_element_type=jnp.float32,
                    )

        return carry

    lax.fori_loop(0, count, step, 0)


def condition_kernel(
    window_ref, extra_ref, ids_ref, theta_ref, white_ref, term_ref, w_ref, xb_ref, yb_ref, mb_ref, li_ref, ld_ref,
    *, reps, sets,
):
    width = window_ref.shape[2]
    count = sets * width // TILE
    blocks = [(ids_ref[i], (ids_ref[sets + i]).astype(jnp.float32)) for i in range(sets)]
    load_set(blocks, window_ref, theta_ref, reps, width, w_ref, xb_ref, yb_ref, mb_ref, count * TILE)
    eliminate(count, (count + 1) * TILE, w_ref, li_ref, ld_ref)
    own = slice((sets - 1) * width, sets * width)
    white = jnp.transpose(w_ref[own, count * TILE : (count + 1) * TILE])[0:reps, :]
    white_ref[...] = white
    logs = ld_ref[count - width // TILE]
    for i in range(count - width // TILE + 1, count):
        logs = logs + ld_ref[i]
    at = lax.broadcasted_iota(jnp.int32, GROUP, 1)
    logdet = 0.5 * jnp.sum(jnp.where(at == 0, logs, 0.0))
    term = -0.5 * jnp.sum(white * white) - reps * logdet
    term_ref[...] = extra_ref[...] + jnp.where(at == 0, term, 0.0)


def predict_kernel(
    window_ref, grid_ref, ids_ref, theta_ref, out_ref, w_ref, xb_ref, yb_ref, mb_ref, li_ref, ld_ref, *, reps, sets
):
    width = window_ref.shape[2]
    points = grid_ref.shape[1]
    count = sets * width // TILE
    blocks = [(ids_ref[i], (ids_ref[sets + i]).astype(jnp.float32)) for i in range(sets)]
    data_at = count * TILE
    load_set(blocks, window_ref, theta_ref, reps, width, w_ref, xb_ref, yb_ref, mb_ref, data_at)
    s2 = theta_ref[0]
    slope = -1.0 / jnp.full((1, TILE), theta_ref[1], jnp.float32)
    grid_at = data_at + TILE
    for c in range(points // TILE):
        lanes = slice(c * TILE, (c + 1) * TILE)
        xr, yr = grid_ref[0:1, lanes], grid_ref[1:2, lanes]
        for r in range(count):
            at = slice(r * TILE, (r + 1) * TILE)
            dx = xb_ref[at, :] - xr
            dy = yb_ref[at, :] - yr
            w_ref[at, grid_at + c * TILE : grid_at + (c + 1) * TILE] = (
                jnp.exp(jnp.sqrt(dx * dx + dy * dy) * slope) * (mb_ref[at, :] * s2)
            )
    eliminate(count, grid_at + points, w_ref, li_ref, ld_ref)
    mean = lax.dot_general(
        w_ref[:, data_at : data_at + TILE],
        w_ref[:, grid_at : grid_at + points],
        (((0,), (0,)), ((), ())),
        precision=HI,
        preferred_element_type=jnp.float32,
    )[0:reps, :]
    shape_g, half_h = theta_ref[3], 0.5 * theta_ref[4]
    scale = theta_ref[5] / jnp.full((1, points), shape_g, jnp.float32)
    out_ref[...] = scale * (jnp.exp(shape_g * mean) - 1.0) * jnp.exp(half_h * mean * mean)


VMEM = pl.BlockSpec(memory_space=pltpu.VMEM)
SMEM = pl.BlockSpec(memory_space=pltpu.SMEM)


def scratch(sets, width, extra):
    sites = sets * width
    return [
        pltpu.VMEM((sites, sites + extra), jnp.float32),
        pltpu.VMEM((sites, TILE), jnp.float32),
        pltpu.VMEM((sites, TILE), jnp.float32),
        pltpu.VMEM((sites, TILE), jnp.float32),
        pltpu.VMEM((TILE, TILE), jnp.float32),
        pltpu.VMEM((sites // TILE,) + GROUP, jnp.float32),
    ]


PARAMS = pltpu.CompilerParams(vmem_limit_bytes=40 * 1024 * 1024)


def body(coords, values, valid, neighbours, grid, sources, theta):
    blocks, _, width = coords.shape
    reps = values.shape[1]
    tiles, _, points = grid.shape
    n_blk = lax.axis_size("blk")
    group = blocks * n_blk
    space_index = lax.axis_index("space")
    first_id = (space_index * n_blk + lax.axis_index("blk")) * blocks
    base = (space_index - HIST) * group
    packed, extra = pl.pallas_call(
        prepare_kernel,
        out_shape=(
            jax.ShapeDtypeStruct((blocks, ROWS, width), jnp.float32),
            jax.ShapeDtypeStruct((blocks,) + GROUP, jnp.float32),
        ),
        in_specs=[VMEM, VMEM, SMEM, SMEM],
        out_specs=(VMEM, VMEM),
        name="prepare",
    )(values, coords, valid, theta)
    grouped = lax.all_gather(packed, "blk", axis=0, tiled=True)
    pieces = [grouped]
    for step in range(1, HIST + 1):
        pieces.insert(0, passed_along(grouped, "space", step))
    window = jnp.concatenate(pieces, axis=0)

    own_ids = first_id + jnp.arange(blocks, dtype=jnp.int32)[:, None]
    cond_ids = jnp.concatenate([neighbours, own_ids], axis=1)

    def listed(ids):
        present = (ids >= 0).astype(jnp.int32)
        return jnp.concatenate([jnp.where(ids >= 0, ids - base, 0), present], axis=1)

    cond_list, pred_list = listed(cond_ids), listed(sources)
    whitened, terms, predicted = [], [], []
    sets = cond_ids.shape[1]
    for index in range(blocks):
        white, term = pl.pallas_call(
            functools.partial(condition_kernel, reps=reps, sets=sets),
            out_shape=(
                jax.ShapeDtypeStruct((reps, width), jnp.float32),
                jax.ShapeDtypeStruct(GROUP, jnp.float32),
            ),
            in_specs=[VMEM, VMEM, SMEM, SMEM],
            out_specs=(VMEM, VMEM),
            scratch_shapes=scratch(sets, width, TILE),
            compiler_params=PARAMS,
            name="condition",
        )(window, extra[index], cond_list[index], theta)
        whitened.append(white)
        terms.append(term)
    sets = sources.shape[1]
    for index in range(tiles):
        predicted.append(
            pl.pallas_call(
                functools.partial(predict_kernel, reps=reps, sets=sets),
                out_shape=jax.ShapeDtypeStruct((reps, points), jnp.float32),
                in_specs=[VMEM, VMEM, SMEM, SMEM],
                out_specs=VMEM,
                scratch_shapes=scratch(sets, width, TILE + points),
                compiler_params=PARAMS,
                name="predict",
            )(window, grid[index], pred_list[index], theta)
        )
    total = sum(terms[1:], terms[0])[0:1]
    total = summed_over(summed_over(total, "blk"), "space")
    loglik = total[0, 0] / (reps * total[0, 1])
    return jnp.stack(whitened), jnp.stack(predicted), loglik


def solution(mesh):
    rows = P(("space", "blk"), None, None)
    return jax.shard_map(
        body,
        mesh=mesh,
        in_specs=(rows, rows, P(("space", "blk")), P(("space", "blk"), None), rows, P(("space", "blk"), None), P()),
        out_specs=(rows, rows, P()),
        check_vma=False,
    )
```

time: 697 us -> 107 us (0.15); the launches traced: 686 us -> 107 us
  other arithmetic: 476 us -> 0.32 us
  local copies, waits for them, and re-layouts: 77.4 us -> 1.93 us
  Pallas kernels: 0 us -> 72.5 us
  matrix products: 61.6 us -> 0 us
  blocking collectives: 43.2 us -> 2.17 us
  between operations: 19.1 us -> 3.76 us
  starting transfers between devices: 8.16 us -> 19.5 us
    another operation x60 -> x0, other arithmetic: 446 us -> none  [the longest x54 297 us: factor_of(): return jnp.linalg.cholesky(matrix)]
    pallas_call x0 -> x3, Pallas kernels: none -> 72.5 us  [the longest x1 40.3 us: body(): pl.pallas_call(functools.partial(condition_kernel, reps=reps, sets=sets),...]
    another operation x61 -> x0, matrix products: 59.4 us -> none  [the longest x24 33.3 us: factor_of(): return jnp.linalg.cholesky(matrix)]
    another operation x58 -> x0, local copies, waits for them, and re-layouts: 52.4 us -> none
    psum x1 -> x0, blocking collectives: 41.3 us -> none  [body(): lax.psum((jnp.sum(terms), jnp.sum(valid.astype(jnp.float32))), ('space',...]
    gather x3 -> x0, local copies, waits for them, and re-layouts: 18.4 us -> none  [the longest x1 17.3 us: condition(): logdiag = jnp.log(jnp.diagonal(factor))[K * width:]]
    div x2 -> x0, other arithmetic: 11.6 us -> none  [factor_of(): return jnp.linalg.cholesky(matrix)]
    ppermute x0 -> x5, starting transfers between devices: none -> 11.4 us  [summed_over(): lax.ppermute(value, axis, [(i, i ^ step) for i in range(count)])]
  transfers between devices with their start and end apart: 2 -> 7, of which waited for: 0 -> 5; matrix products, arithmetic and copies ran while one was open for 2% -> 0% of each run, Pallas kernels for 0% -> 28%
where the time goes in v1:
time: 107 us
  Pallas kernels  72.5 us (68%)
  starting transfers between devices  19.5 us (18%)
  waiting for transfers between devices  6.79 us (6%)
  between operations  3.76 us (4%)
  blocking collectives  2.17 us (2%)
  local copies, waits for them, and re-layouts  1.93 us (2%)
    pallas_call x1, Pallas kernels, body(): pl.pallas_call(functools.partial(condition_kernel, reps=reps, sets=sets),...  40.3 us
    pallas_call x1, Pallas kernels, body(): pl.pallas_call(functools.partial(predict_kernel, reps=reps, sets=sets), o...  30.5 us
    ppermute x5, starting transfers between devices, summed_over(): lax.ppermute(value, axis, [(i, i ^ step) for i in range(count)])  11.4 us
    ppermute x2, starting transfers between devices, passed_along(): lax.ppermute(value, axis, [(source, source + steps) for source in range(i...  8.16 us
    ppermute x5, waiting for transfers between devices, summed_over(): lax.ppermute(value, axis, [(i, i ^ step) for i in range(count)])  5.66 us
    all_gather x1, blocking collectives, body(): grouped = lax.all_gather(packed, 'blk', axis=0, tiled=True)  2.17 us
  transfers between devices with their start and end apart: 7, of which 5 were waited for; matrix products, arithmetic and copies ran while one was open for 0% of the time, Pallas kernels for 28%

profile of v1, /device:TPU:0, one launch (start us, length us, event | category | flops | bytes accessed | tf_op | source)
XLA Modules:
  0.0 107.0 jit_solution(4762995031383634148)
XLA Ops:
  1.3 1.7 %prepare.1 = (f32[1,40,256]{2,1,0:T(8,128)}, f32[1,8,128]{2,1,0:T(8,128)}) custom-call(f32[1,32,256]{2,1,0:T(8,128)} %values_ref.1, f32[1,2,256]{2,1,0:T(2,128)} %coords_ref.1, s32[1]{0:T(128)S(6)} %copy.12.valid_ref, f32[6]{0:T(128)} %theta_ref.5), custom_call_target="tpu_custom_call" | custom-call | tf_op jit(solution)/shard_map/prepare/pallas_call | solution.py:284
  3.0 2.2 %all_gather.3 = f32[2,40,256]{2,1,0:T(8,128)S(1)} all-gather(f32[1,40,256]{2,1,0:T(8,128)} %get-tuple-element.7), channel_id=1, replica_groups=mesh['space'=16,'blk'=2] {'blk'}, dimensions={0}, use_global_device_ids=true | all-gather | bytes 122880 | tf_op jit(solution)/shard_map/all_gather | solution.py:294
  5.2 4.8 %collective-permute-start = (f32[2,40,256]{2,1,0:T(8,128)S(1)}, f32[2,40,256]{2,1,0:T(8,128)S(1)}, u32[]{:S(2)}, u32[]{:S(2)}) collective-permute-start(f32[2,40,256]{2,1,0:T(8,128)S(1)} %all_gather.3), channel_id=1, source_target_pairs={{0,4},{2,6},{4,8},{6,10},{8,12},{10,14},{12,16},{14,18},{16,20},{1... | collective-permute-start | bytes 245768 | tf_op jit(solution)/shard_map/ppermute | solution.py:22
  10.0 3.4 %collective-permute-start.1 = (f32[2,40,256]{2,1,0:T(8,128)S(1)}, f32[2,40,256]{2,1,0:T(8,128)S(1)}, u32[]{:S(2)}, u32[]{:S(2)}) collective-permute-start(f32[2,40,256]{2,1,0:T(8,128)S(1)} %all_gather.3), channel_id=1, source_target_pairs={{0,2},{2,4},{4,6},{6,8},{8,10},{10,12},{12,14},{14,16},{16,18},{18... | collective-permute-start | bytes 245768 | tf_op jit(solution)/shard_map/ppermute | solution.py:22
  13.4 0.0 copy-start.3
  13.4 0.6 copy-done.3
  14.0 0.1 compare_convert_fusion.1
  14.1 0.1 compare_select_fusion.1
  14.2 0.1 add_bitcast_fusion.ids_ref
  14.3 0.0 collective-permute-done
  14.3 1.1 %collective-permute-done.1 = f32[2,40,256]{2,1,0:T(8,128)S(1)} collective-permute-done((f32[2,40,256]{2,1,0:T(8,128)S(1)}, f32[2,40,256]{2,1,0:T(8,128)S(1)}, u32[]{:S(2)}, u32[]{:S(2)}) %collective-permute-start.1) | collective-permute-done | bytes 81952 | tf_op jit(solution)/shard_map/ppermute | solution.py:22
  15.4 0.0 copy-start.1
  15.4 0.0 copy-start
  15.4 0.7 copy-done.1
  16.1 0.0 copy-done
  16.1 40.3 %condition.1 = (f32[32,256]{1,0:T(8,128)}, f32[8,128]{1,0:T(8,128)S(1)}) custom-call(f32[6,40,256]{2,1,0:T(8,128)S(1)} %constant_dynamic-update-slice_fusion.window_ref, f32[8,128]{1,0:T(8,128)S(1)} %bitcast.10, s32[8]{0:T(128)S(1)} %add_bitcast_fusion.ids_ref, f32[6]{0:T(128)S(1)} %copy-done), custom_call_target="tpu_custom_call" | custom-call | tf_op jit(solution)/shard_map/condition/pallas_call | solution.py:311
  56.4 0.0 collective-permute-start.2
  56.4 1.1 %collective-permute-done.2 = f32[1,128]{1,0:T(1,128)S(1)} collective-permute-done((f32[1,128]{1,0:T(1,128)S(1)}, f32[1,128]{1,0:T(1,128)S(1)}, u32[]{:S(2)}, u32[]{:S(2)}) %collective-permute-start.2) | collective-permute-done | bytes 544 | tf_op jit(solution)/shard_map/ppermute | solution.py:35
  57.5 0.0 copy-start.4
  57.5 2.4 %collective-permute-start.3 = (f32[1,128]{1,0:T(1,128)S(1)}, f32[1,128]{1,0:T(1,128)S(1)}, u32[]{:S(2)}, u32[]{:S(2)}) collective-permute-start(f32[1,128]{1,0:T(1,128)S(1)} %slice_add_fusion), channel_id=1, source_target_pairs={{0,2},{2,0},{4,6},{6,4},{8,10},{10,8},{12,14},{14,12},{16,18},{18,... | collective-permute-start | bytes 1544 | tf_op jit(solution)/shard_map/ppermute | solution.py:35
  59.9 1.5 %collective-permute-done.3 = f32[1,128]{1,0:T(1,128)S(1)} collective-permute-done((f32[1,128]{1,0:T(1,128)S(1)}, f32[1,128]{1,0:T(1,128)S(1)}, u32[]{:S(2)}, u32[]{:S(2)}) %collective-permute-start.3) | collective-permute-done | bytes 544 | tf_op jit(solution)/shard_map/ppermute | solution.py:35
  61.4 3.0 %collective-permute-start.4 = (f32[1,128]{1,0:T(1,128)S(1)}, f32[1,128]{1,0:T(1,128)S(1)}, u32[]{:S(2)}, u32[]{:S(2)}) collective-permute-start(f32[1,128]{1,0:T(1,128)S(1)} %add.22), channel_id=1, source_target_pairs={{0,4},{2,6},{4,0},{6,2},{8,12},{10,14},{12,8},{14,10},{16,20},{18,... | collective-permute-start | bytes 1544 | tf_op jit(solution)/shard_map/ppermute | solution.py:35
  64.4 0.0 copy-done.4
  64.4 1.5 %collective-permute-done.4 = f32[1,128]{1,0:T(1,128)S(1)} collective-permute-done((f32[1,128]{1,0:T(1,128)S(1)}, f32[1,128]{1,0:T(1,128)S(1)}, u32[]{:S(2)}, u32[]{:S(2)}) %collective-permute-start.4) | collective-permute-done | bytes 544 | tf_op jit(solution)/shard_map/ppermute | solution.py:35
  65.9 3.0 %collective-permute-start.5 = (f32[1,128]{1,0:T(1,128)S(1)}, f32[1,128]{1,0:T(1,128)S(1)}, u32[]{:S(2)}, u32[]{:S(2)}) collective-permute-start(f32[1,128]{1,0:T(1,128)S(1)} %add.23), channel_id=1, source_target_pairs={{0,8},{2,10},{4,12},{6,14},{8,0},{10,2},{12,4},{14,6},{16,24},{18,... | collective-permute-start | bytes 1544 | tf_op jit(solution)/shard_map/ppermute | solution.py:35
  68.9 1.5 %collective-permute-done.5 = f32[1,128]{1,0:T(1,128)S(1)} collective-permute-done((f32[1,128]{1,0:T(1,128)S(1)}, f32[1,128]{1,0:T(1,128)S(1)}, u32[]{:S(2)}, u32[]{:S(2)}) %collective-permute-start.5) | collective-permute-done | bytes 544 | tf_op jit(solution)/shard_map/ppermute | solution.py:35
  70.4 3.0 %collective-permute-start.6 = (f32[1,128]{1,0:T(1,128)S(1)}, f32[1,128]{1,0:T(1,128)S(1)}, u32[]{:S(2)}, u32[]{:S(2)}) collective-permute-start(f32[1,128]{1,0:T(1,128)S(1)} %add.24), channel_id=1, source_target_pairs={{0,16},{2,18},{4,20},{6,22},{8,24},{10,26},{12,28},{14,30},{16,0},... | collective-permute-start | bytes 1544 | tf_op jit(solution)/shard_map/ppermute | solution.py:35
  73.4 0.1 add_bitcast_fusion.1.ids_ref
  73.5 0.0 copy-done.2
  73.5 30.5 %predict.1 = f32[32,256]{1,0:T(8,128)} custom-call(f32[6,40,256]{2,1,0:T(8,128)S(1)} %constant_dynamic-update-slice_fusion.window_ref, f32[2,256]{1,0:T(2,128)S(1)} %bitcast.11, s32[6]{0:T(128)S(1)} %add_bitcast_fusion.1.ids_ref, f32[6]{0:T(128)S(1)} %copy-done), custom_call_target="tpu_custom_call" | custom-call | tf_op jit(solution)/shard_map/predict/pallas_call | solution.py:328
  104.0 0.0 collective-permute-done.6
  104.0 0.6 fusion
  (12 shorter events, 0.0 us)
Async XLA Ops:
  5.2 9.1 %collective-permute-start = (f32[2,40,256]{2,1,0:T(8,128)S(1)}, f32[2,40,256]{2,1,0:T(8,128)S(1)}, u32[]{:S(2)}, u32[]{:S(2)}) collective-permute-start(f32[2,40,256]{2,1,0:T(8,128)S(1)} %all_gather.3), channel_id=1, source_target_pairs={{0,4},{2,6},{4,8},{6,10},{8,12},{10,14},{12,16},{14,18},{16,20},{1... | collective-permute-start | bytes 245768 | tf_op jit(solution)/shard_map/ppermute | solution.py:22
  10.0 5.4 %collective-permute-start.1 = (f32[2,40,256]{2,1,0:T(8,128)S(1)}, f32[2,40,256]{2,1,0:T(8,128)S(1)}, u32[]{:S(2)}, u32[]{:S(2)}) collective-permute-start(f32[2,40,256]{2,1,0:T(8,128)S(1)} %all_gather.3), channel_id=1, source_target_pairs={{0,2},{2,4},{4,6},{6,8},{8,10},{10,12},{12,14},{14,16},{16,18},{18... | collective-permute-start | bytes 245768 | tf_op jit(solution)/shard_map/ppermute | solution.py:22
  13.4 0.7 copy-start.3
  15.4 0.7 copy-start.1
  15.4 0.7 copy-start
  56.4 1.1 %collective-permute-start.2 = (f32[1,128]{1,0:T(1,128)S(1)}, f32[1,128]{1,0:T(1,128)S(1)}, u32[]{:S(2)}, u32[]{:S(2)}) collective-permute-start(f32[1,128]{1,0:T(1,128)S(1)} %slice.9), channel_id=1, source_target_pairs={{0,1},{1,0},{2,3},{3,2},{4,5},{5,4},{6,7},{7,6},{8,9},{9,8},{10,11... | collective-permute-start | bytes 1544 | tf_op jit(solution)/shard_map/ppermute | solution.py:35
  57.5 6.9 %copy-start.4 = (s32[1,3]{1,0:T(1,128)S(1)}, s32[1,3]{1,0:T(1,128)}, u32[]{:S(2)}) copy-start(s32[1,3]{1,0:T(1,128)} %param.12) | copy-start | bytes 40
  57.5 3.9 %collective-permute-start.3 = (f32[1,128]{1,0:T(1,128)S(1)}, f32[1,128]{1,0:T(1,128)S(1)}, u32[]{:S(2)}, u32[]{:S(2)}) collective-permute-start(f32[1,128]{1,0:T(1,128)S(1)} %slice_add_fusion), channel_id=1, source_target_pairs={{0,2},{2,0},{4,6},{6,4},{8,10},{10,8},{12,14},{14,12},{16,18},{18,... | collective-permute-start | bytes 1544 | tf_op jit(solution)/shard_map/ppermute | solution.py:35
  61.4 4.5 %collective-permute-start.4 = (f32[1,128]{1,0:T(1,128)S(1)}, f32[1,128]{1,0:T(1,128)S(1)}, u32[]{:S(2)}, u32[]{:S(2)}) collective-permute-start(f32[1,128]{1,0:T(1,128)S(1)} %add.22), channel_id=1, source_target_pairs={{0,4},{2,6},{4,0},{6,2},{8,12},{10,14},{12,8},{14,10},{16,20},{18,... | collective-permute-start | bytes 1544 | tf_op jit(solution)/shard_map/ppermute | solution.py:35
  65.9 4.5 %collective-permute-start.5 = (f32[1,128]{1,0:T(1,128)S(1)}, f32[1,128]{1,0:T(1,128)S(1)}, u32[]{:S(2)}, u32[]{:S(2)}) collective-permute-start(f32[1,128]{1,0:T(1,128)S(1)} %add.23), channel_id=1, source_target_pairs={{0,8},{2,10},{4,12},{6,14},{8,0},{10,2},{12,4},{14,6},{16,24},{18,... | collective-permute-start | bytes 1544 | tf_op jit(solution)/shard_map/ppermute | solution.py:35
  70.4 3.1 %copy-start.2 = (f32[1,2,256]{2,1,0:T(2,128)S(1)}, f32[1,2,256]{2,1,0:T(2,128)}, u32[]{:S(2)}) copy-start(f32[1,2,256]{2,1,0:T(2,128)} %param.11) | copy-start | bytes 6148
  70.4 33.6 %collective-permute-start.6 = (f32[1,128]{1,0:T(1,128)S(1)}, f32[1,128]{1,0:T(1,128)S(1)}, u32[]{:S(2)}, u32[]{:S(2)}) collective-permute-start(f32[1,128]{1,0:T(1,128)S(1)} %add.24), channel_id=1, source_target_pairs={{0,16},{2,18},{4,20},{6,22},{8,24},{10,26},{12,28},{14,30},{16,0},... | collective-permute-start | bytes 1544 | tf_op jit(solution)/shard_map/ppermute | solution.py:35

commit v2 on v1

v2 whole, which is shorter than its diff:
```python
import functools
import math

import jax
import jax.numpy as jnp
from jax import lax
from jax.experimental import pallas as pl
from jax.experimental.pallas import tpu as pltpu
from jax.sharding import PartitionSpec as P

HIST = 2
NEWTON = 8
TILE = 128
GROUP = (8, 128)
ROWS = 40
HI = lax.Precision.HIGHEST


def passed_along(value, axis, steps):
    count = lax.axis_size(axis)
    initial, last = (max(0, -steps), min(count, count - steps))
    return lax.ppermute(value, axis, [(source, source + steps) for source in range(initial, last)])


def summed_over(value, axis):
    count = lax.axis_size(axis)
    if count & (count - 1):
        total = value
        for _ in range(count - 1):
            value = lax.ppermute(value, axis, [(i, (i + 1) % count) for i in range(count)])
            total = total + value
        return total
    step = 1
    while step < count:
        value = value + lax.ppermute(value, axis, [(i, i ^ step) for i in range(count)])
        step *= 2
    return value


def prepare_kernel(values_ref, coords_ref, valid_ref, theta_ref, packed_ref, extra_ref):
    reps, width = values_ref.shape[1], values_ref.shape[2]
    shape_g, shape_h, omega = theta_ref[3], theta_ref[4], theta_ref[5]
    one = jnp.ones((1, width), jnp.float32)
    inv_g = 1.0 / (one * shape_g)
    inv_omega = 1.0 / (one * omega)
    half_h = 0.5 * shape_h

    def parts(point):
        grow = jnp.exp(shape_g * point)
        heavy = jnp.exp(half_h * point * point)
        value = (grow - 1.0) * inv_g * heavy
        return value, grow * heavy + shape_h * point * value

    for index in range(values_ref.shape[0]):
        lane = lax.broadcasted_iota(jnp.int32, (1, width), 1)
        mask = (lane < valid_ref[index]).astype(jnp.float32)
        target = values_ref[index] * inv_omega
        point = jnp.zeros_like(target)
        for _ in range(NEWTON):
            value, slope = parts(point)
            point = point - (value - target) / slope
        _, slope = parts(point)
        logjac = jnp.log(omega * slope) * mask
        packed_ref[index, 0:reps, :] = point * mask
        packed_ref[index, reps : reps + 2, :] = coords_ref[index]
        packed_ref[index, reps + 2 : reps + 3, :] = mask
        packed_ref[index, reps + 3 :, :] = jnp.zeros((ROWS - reps - 3, width), jnp.float32)
        live = jnp.sum(mask)
        part = -jnp.sum(logjac) - 0.5 * reps * math.log(2.0 * math.pi) * live
        at = lax.broadcasted_iota(jnp.int32, GROUP, 1)
        extra_ref[index] = jnp.where(at == 0, part, jnp.where(at == 1, live, 0.0))


def over_sublanes(x, j):
    return jnp.broadcast_to(x[j : j + 1, :], GROUP)


def over_lanes(x, j):
    return jnp.broadcast_to(x[:, j : j + 1], GROUP)


def tree_sum(terms):
    terms = list(terms)
    while len(terms) > 1:
        odd = [terms[-1]] if len(terms) % 2 else []
        terms = [a + b for a, b in zip(terms[::2], terms[1::2])] + odd
    return terms[0]


def eliminate_groups(rows, out, logs, lo, hi, cols_ref):
    sub = lax.broadcasted_iota(jnp.int32, GROUP, 0)
    lane = lax.broadcasted_iota(jnp.int32, GROUP, 1)
    unit = [jnp.where(sub == j, 1.0, 0.0).astype(jnp.float32) for j in range(8)]

    def extract(p):
        for j in range(8):
            for q in range(p + 1, hi):
                cols_ref[p % 2, (q - lo) * 8 + j] = over_lanes(rows[q], 8 * p + j)

    diag = [over_lanes(rows[lo], 8 * lo + j) for j in range(8)]
    extract(lo)
    yield
    for p in range(lo, hi):
        panel = (lane >= 8 * p) & (lane < 8 * p + 8)
        start = jnp.where(panel, jnp.where(lane == sub + 8 * p, 1.0, 0.0), rows[p])
        solved, product, kept = start, None, []
        for j in range(0, 8, 2):
            x, y = diag[j], diag[j + 1]
            a, b, c = over_sublanes(x, j), over_sublanes(x, j + 1), over_sublanes(y, j + 1)
            det = a * c - b * b
            recip = 1.0 / det
            x, y = x - unit[j], y - unit[j + 1]
            nx, ny = c * x - b * y, a * y - b * x
            for k in range(j + 2, 8):
                u, v = over_sublanes(diag[k], j), over_sublanes(diag[k], j + 1)
                diag[k] = diag[k] - (nx * u + ny * v) * recip
            solved = solved - (nx * over_sublanes(solved, j) + ny * over_sublanes(solved, j + 1)) * recip
            kept.append((a, b, recip, nx, ny))
            product = det if product is None else product * det
            yield
        if p + 1 < hi:
            across = [over_sublanes(solved, j) for j in range(8)]

            def update(q):
                moved = tree_sum([cols_ref[p % 2, (q - lo) * 8 + j] * across[j] for j in range(8)])
                rows[q] = jnp.where(panel, 0.0, rows[q]) - moved

            update(p + 1)
            diag = [over_lanes(rows[p + 1], 8 * (p + 1) + j) for j in range(8)]
            yield
            for q in range(p + 2, hi):
                update(q)
            extract(p + 1)
        lower = start
        scale, fix = jnp.zeros(GROUP, jnp.float32), jnp.zeros(GROUP, jnp.float32)
        for j in range(0, 8, 2):
            a, b, recip, nx, ny = kept[j // 2]
            inv_a = 1.0 / a
            u = over_sublanes(lower, j)
            fix = jnp.where(sub == j + 1, (b * inv_a) * u, fix)
            scale = jnp.where(sub == j, inv_a, jnp.where(sub == j + 1, a * recip, scale))
            if j < 6:
                v = over_sublanes(lower, j + 1)
                lower = lower - jnp.where(sub > j + 1, (nx * u + ny * v) * recip, 0.0)
        out[p] = (lower - fix) * jnp.sqrt(scale)
        logs[p] = jnp.log(product)
        yield


def factor_tile(rows, cols_ref, inverse_ref, logs_ref, part=8):
    count = TILE // 8
    rows, out, logs = list(rows), [None] * count, [None] * count
    lane = lax.broadcasted_iota(jnp.int32, GROUP, 1)
    for lo in range(0, count, part):
        hi = lo + part
        yield from eliminate_groups(rows, out, logs, lo, hi, cols_ref)
        for q in range(lo, hi):
            inverse_ref[8 * q : 8 * q + 8, :] = jnp.where(lane < 8 * q + 8, out[q], 0.0)
        if hi < count:
            top = [jnp.where((lane < 8 * q + 8) | (lane >= 8 * hi), out[q], 0.0) for q in range(lo, hi)]
            top = jnp.concatenate(top, axis=0)
            moved = lax.dot_general(
                top[:, 8 * hi :], top, (((0,), (0,)), ((), ())), precision=HI, preferred_element_type=jnp.float32
            )
            done = (lane >= 8 * lo) & (lane < 8 * hi)
            for q in range(hi, count):
                i = 8 * (q - hi)
                rows[q] = jnp.where(done, 0.0, rows[q]) - moved[i : i + 8]
            yield
    logs_ref[...] = tree_sum(logs)


def take_turns(streams, lead):
    for i, stream in enumerate(streams):
        for _ in range(lead * (len(streams) - 1 - i)):
            next(stream, None)
    live = list(streams)
    while live:
        for stream in list(live):
            try:
                next(stream)
            except StopIteration:
                live.remove(stream)


def decay(dx, dy, slope):
    square = jnp.maximum(dx * dx + dy * dy, 1e-30)
    return jnp.exp(square * lax.rsqrt(square) * slope)


def load_set(blocks, window_ref, theta_ref, reps, width, w_ref, xb_ref, yb_ref, mb_ref, data_at):
    s2, rho, nug = theta_ref[0], theta_ref[1], theta_ref[2]
    slope = -1.0 / jnp.full((1, TILE), rho, jnp.float32)
    per = width // TILE
    for n, (index, present) in enumerate(blocks):
        block = window_ref[index]
        full = jnp.concatenate([block, jnp.zeros((TILE - ROWS, width), jnp.float32)], axis=0)
        turned = jnp.transpose(full)
        at = slice(n * width, (n + 1) * width)
        xb_ref[at, :] = jnp.broadcast_to(turned[:, reps : reps + 1], (width, TILE))
        yb_ref[at, :] = jnp.broadcast_to(turned[:, reps + 1 : reps + 2], (width, TILE))
        mb_ref[at, :] = jnp.broadcast_to(turned[:, reps + 2 : reps + 3] * present, (width, TILE))
        w_ref[at, data_at : data_at + TILE] = turned * present
    sub = lax.broadcasted_iota(jnp.int32, (TILE, TILE), 0)
    lane = lax.broadcasted_iota(jnp.int32, (TILE, TILE), 1)
    for n, (index, present) in enumerate(blocks):
        for part in range(per):
            c = n * per + part
            lanes = slice(part * TILE, (part + 1) * TILE)
            xr = window_ref[index, reps : reps + 1, lanes]
            yr = window_ref[index, reps + 1 : reps + 2, lanes]
            mr = window_ref[index, reps + 2 : reps + 3, lanes] * present

            def tile(at):
                dx = xb_ref[at, :] - xr
                dy = yb_ref[at, :] - yr
                return decay(dx, dy, slope) * (mb_ref[at, :] * (mr * s2))

            for r in range(c):
                at = slice(r * TILE, (r + 1) * TILE)
                w_ref[at, c * TILE : (c + 1) * TILE] = tile(at)
            at = slice(c * TILE, (c + 1) * TILE)
            w_ref[at, at] = jnp.where(sub == lane, mr * (s2 + nug) + (1.0 - mr), tile(at))


def thirds(x):
    high = x.astype(jnp.bfloat16)
    rest = x - high.astype(jnp.float32)
    mid = rest.astype(jnp.bfloat16)
    return high, mid, (rest - mid.astype(jnp.float32)).astype(jnp.bfloat16)


def left_parts(x):
    h, m, l = thirds(x)
    return jnp.concatenate([h, h, m, h, l, m], axis=1)


def right_parts(x):
    h, m, l = thirds(x)
    return jnp.concatenate([h, m, h, l, h, m], axis=0)


def product(left, right):
    return lax.dot(left, right, preferred_element_type=jnp.float32)


def eliminate(systems, lo, hi, cols_ref, li_ref):
    def step(k, carry):
        off = pl.multiple_of(k * TILE, TILE)
        streams = []
        for i, (w_ref, logs_ref, _, _) in enumerate(systems):
            rows = [w_ref[pl.ds(off + 8 * q, 8), pl.ds(off, TILE)] for q in range(TILE // 8)]
            streams.append(factor_tile(rows, cols_ref.at[i], li_ref.at[i], logs_ref.at[k]))
        take_turns(streams, 3)
        for kk in range(lo, hi):

            @pl.when(k == kk)
            def _():
                at = slice(kk * TILE, (kk + 1) * TILE)
                start = (kk + 1) * TILE
                rights, lefts = [], []
                for i, (w_ref, _, tiles, total) in enumerate(systems):
                    solved = product(left_parts(li_ref[i]), right_parts(w_ref[at, start:total]))
                    w_ref[at, start:total] = solved
                    if kk + 1 < tiles:
                        rights.append(right_parts(solved))
                        lefts.append(left_parts(jnp.transpose(solved[:, : tiles * TILE - start])))
                row = kk + 1
                while row < max(system[2] for system in systems):
                    end = row + 2 - row % 2
                    for i, (w_ref, _, tiles, total) in enumerate(systems):
                        if row < tiles:
                            first, last = row * TILE, end * TILE
                            w_ref[first:last, first:total] -= product(
                                lefts[i][first - start : last - start], rights[i][:, first - start :]
                            )
                    row = end

        return carry

    lax.fori_loop(lo, hi, step, 0)


def both_kernel(
    window_ref, extra_ref, cond_ref, pred_ref, grid_ref, theta_ref, white_ref, term_ref, out_ref,
    wc_ref, wp_ref, xb_ref, yb_ref, mb_ref, cols_ref, li_ref, lc_ref, lp_ref, *, reps, sets, sources,
):
    width, points = window_ref.shape[2], grid_ref.shape[1]

    def listed(ref, number):
        return [(ref[i], ref[number + i].astype(jnp.float32)) for i in range(number)]

    count, data_at = sources * width // TILE, sources * width
    load_set(listed(pred_ref, sources), window_ref, theta_ref, reps, width, wp_ref, xb_ref, yb_ref, mb_ref, data_at)
    slope = -1.0 / jnp.full((1, TILE), theta_ref[1], jnp.float32)
    grid_at = data_at + TILE
    for c in range(points // TILE):
        lanes = slice(c * TILE, (c + 1) * TILE)
        xr, yr = grid_ref[0:1, lanes], grid_ref[1:2, lanes]
        for r in range(count):
            at = slice(r * TILE, (r + 1) * TILE)
            dx = xb_ref[at, :] - xr
            dy = yb_ref[at, :] - yr
            wp_ref[at, grid_at + c * TILE : grid_at + (c + 1) * TILE] = (
                decay(dx, dy, slope) * (mb_ref[at, :] * theta_ref[0])
            )
    predicting = (wp_ref, lp_ref, count, grid_at + points)
    count, data_at = sets * width // TILE, sets * width
    load_set(listed(cond_ref, sets), window_ref, theta_ref, reps, width, wc_ref, xb_ref, yb_ref, mb_ref, data_at)
    conditioning = (wc_ref, lc_ref, count, data_at + TILE)
    both = min(predicting[2], count)
    eliminate([conditioning, predicting], 0, both, cols_ref, li_ref)
    for system in (conditioning, predicting):
        if system[2] > both:
            eliminate([system], both, system[2], cols_ref, li_ref)

    own = slice((sets - 1) * width, sets * width)
    white = jnp.transpose(wc_ref[own, data_at : data_at + TILE])[0:reps, :]
    white_ref[...] = white
    logs = tree_sum([lc_ref[i] for i in range(count - width // TILE, count)])
    at = lax.broadcasted_iota(jnp.int32, GROUP, 1)
    sub = lax.broadcasted_iota(jnp.int32, GROUP, 0)
    logdet = 0.5 * jnp.sum(jnp.where((at == 0) & (sub == 0), logs, 0.0))
    term = -0.5 * jnp.sum(white * white) - reps * logdet
    term_ref[...] = extra_ref[...] + jnp.where(at == 0, term, 0.0)

    mean = lax.dot_general(
        wp_ref[:, sources * width : sources * width + TILE],
        wp_ref[:, grid_at : grid_at + points],
        (((0,), (0,)), ((), ())),
        precision=HI,
        preferred_element_type=jnp.float32,
    )[0:reps, :]
    shape_g, half_h = theta_ref[3], 0.5 * theta_ref[4]
    scale = theta_ref[5] / jnp.full((1, points), shape_g, jnp.float32)
    out_ref[...] = scale * (jnp.exp(shape_g * mean) - 1.0) * jnp.exp(half_h * mean * mean)


VMEM = pl.BlockSpec(memory_space=pltpu.VMEM)
SMEM = pl.BlockSpec(memory_space=pltpu.SMEM)


PARAMS = pltpu.CompilerParams(vmem_limit_bytes=40 * 1024 * 1024)


def body(coords, values, valid, neighbours, grid, sources, theta):
    blocks, _, width = coords.shape
    reps = values.shape[1]
    tiles, _, points = grid.shape
    n_blk = lax.axis_size("blk")
    group = blocks * n_blk
    space_index = lax.axis_index("space")
    first_id = (space_index * n_blk + lax.axis_index("blk")) * blocks
    base = (space_index - HIST) * group
    packed, extra = pl.pallas_call(
        prepare_kernel,
        out_shape=(
            jax.ShapeDtypeStruct((blocks, ROWS, width), jnp.float32),
            jax.ShapeDtypeStruct((blocks,) + GROUP, jnp.float32),
        ),
        in_specs=[VMEM, VMEM, SMEM, SMEM],
        out_specs=(VMEM, VMEM),
        name="prepare",
    )(values, coords, valid, theta)
    grouped = lax.all_gather(packed, "blk", axis=0, tiled=True)
    pieces = [grouped]
    for step in range(1, HIST + 1):
        pieces.insert(0, passed_along(grouped, "space", step))
    window = jnp.concatenate(pieces, axis=0)

    own_ids = first_id + jnp.arange(blocks, dtype=jnp.int32)[:, None]
    cond_ids = jnp.concatenate([neighbours, own_ids], axis=1)

    def listed(ids):
        present = (ids >= 0).astype(jnp.int32)
        return jnp.concatenate([jnp.where(ids >= 0, ids - base, 0), present], axis=1)

    cond_list, pred_list = listed(cond_ids), listed(sources)
    sets, listed_sources = cond_ids.shape[1], sources.shape[1]
    whitened, terms, predicted = [], [], []
    sites, near = sets * width, listed_sources * width
    wide = max(sites, near)
    for index in range(blocks):
        white, term, field = pl.pallas_call(
            functools.partial(both_kernel, reps=reps, sets=sets, sources=listed_sources),
            out_shape=(
                jax.ShapeDtypeStruct((reps, width), jnp.float32),
                jax.ShapeDtypeStruct(GROUP, jnp.float32),
                jax.ShapeDtypeStruct((reps, points), jnp.float32),
            ),
            in_specs=[VMEM, VMEM, SMEM, SMEM, VMEM, SMEM],
            out_specs=(VMEM, VMEM, VMEM),
            scratch_shapes=[
                pltpu.VMEM((sites, sites + TILE), jnp.float32),
                pltpu.VMEM((near, near + TILE + points), jnp.float32),
                pltpu.VMEM((wide, TILE), jnp.float32),
                pltpu.VMEM((wide, TILE), jnp.float32),
                pltpu.VMEM((wide, TILE), jnp.float32),
                pltpu.VMEM((2, 2, TILE) + GROUP, jnp.float32),
                pltpu.VMEM((2, TILE, TILE), jnp.float32),
                pltpu.VMEM((sites // TILE,) + GROUP, jnp.float32),
                pltpu.VMEM((near // TILE,) + GROUP, jnp.float32),
            ],
            compiler_params=PARAMS,
            name="both",
        )(window, extra[index], cond_list[index], pred_list[index], grid[index], theta)
        whitened.append(white)
        terms.append(term)
        predicted.append(field)
    total = sum(terms[1:], terms[0])[0:1]
    total = summed_over(summed_over(total, "blk"), "space")
    loglik = total[0, 0] / (reps * total[0, 1])
    return jnp.stack(whitened), jnp.stack(predicted), loglik


def solution(mesh):
    rows = P(("space", "blk"), None, None)
    return jax.shard_map(
        body,
        mesh=mesh,
        in_specs=(rows, rows, P(("space", "blk")), P(("space", "blk"), None), rows, P(("space", "blk"), None), P()),
        out_specs=(rows, rows, P()),
        check_vma=False,
    )
```

time: 107 us -> 84.9 us (0.79)
  Pallas kernels: 72.5 us -> 49.6 us
  starting transfers between devices: 19.5 us -> 18 us
  waiting for transfers between devices: 6.79 us -> 8.2 us
    pallas_call x2 -> x1, Pallas kernels: 70.8 us -> 47.8 us  [body(): pl.pallas_call(functools.partial(both_kernel, reps=reps, sets=sets, sourc...]
    ppermute x5, waiting for transfers between devices: 5.66 us -> 7.72 us  [summed_over(): lax.ppermute(value, axis, [(i, i ^ step) for i in range(count)])]
    ppermute x5, starting transfers between devices: 11.4 us -> 9.88 us  [summed_over(): lax.ppermute(value, axis, [(i, i ^ step) for i in range(count)])]
  transfers between devices with their start and end apart: 7 -> 7, of which waited for: 5 -> 6; matrix products, arithmetic and copies ran while one was open for 0% -> 0% of each run, Pallas kernels for 28% -> 0%
where the time goes in v2:
time: 84.9 us; the launch traced here: 84.6 us
  Pallas kernels  49.6 us (58%)
  starting transfers between devices  18 us (21%)
  waiting for transfers between devices  8.2 us (10%)
  between operations  3.76 us (4%)
  local copies, waits for them, and re-layouts  2.5 us (3%)
  blocking collectives  2.17 us (3%)
    pallas_call x1, Pallas kernels, body(): pl.pallas_call(functools.partial(both_kernel, reps=reps, sets=sets, sourc...  47.8 us
    ppermute x5, starting transfers between devices, summed_over(): lax.ppermute(value, axis, [(i, i ^ step) for i in range(count)])  9.88 us
    ppermute x2, starting transfers between devices, passed_along(): lax.ppermute(value, axis, [(source, source + steps) for source in range(i...  8.16 us
    ppermute x5, waiting for transfers between devices, summed_over(): lax.ppermute(value, axis, [(i, i ^ step) for i in range(count)])  7.72 us
    all_gather x1, blocking collectives, body(): grouped = lax.all_gather(packed, 'blk', axis=0, tiled=True)  2.17 us
    unnamed x10, local copies, waits for them, and re-layouts  1.91 us
    pallas_call x1, Pallas kernels, body(): pl.pallas_call(prepare_kernel, out_shape=(jax.ShapeDtypeStruct((blocks, R...  1.74 us
  transfers between devices with their start and end apart: 7, of which 6 were waited for; matrix products, arithmetic and copies ran while one was open for 0% of the time, Pallas kernels for 0%

profile of v2, /device:TPU:0, one launch (start us, length us, event | category | flops | bytes accessed | tf_op | source)
XLA Modules:
  0.0 84.6 jit_solution(11635437744236963144)
XLA Ops:
  1.3 1.7 %prepare.1 = (f32[1,40,256]{2,1,0:T(8,128)}, f32[1,8,128]{2,1,0:T(8,128)}) custom-call(f32[1,32,256]{2,1,0:T(8,128)} %values_ref.1, f32[1,2,256]{2,1,0:T(2,128)} %coords_ref.1, s32[1]{0:T(128)S(6)} %copy.10.valid_ref, f32[6]{0:T(128)} %theta_ref.3), custom_call_target="tpu_custom_call" | custom-call | tf_op jit(solution)/shard_map/prepare/pallas_call | solution.py:355
  3.0 2.2 %all_gather.3 = f32[2,40,256]{2,1,0:T(8,128)S(1)} all-gather(f32[1,40,256]{2,1,0:T(8,128)} %get-tuple-element.8), channel_id=1, replica_groups=mesh['space'=16,'blk'=2] {'blk'}, dimensions={0}, use_global_device_ids=true | all-gather | bytes 122880 | tf_op jit(solution)/shard_map/all_gather | solution.py:365
  5.2 4.7 %collective-permute-start.1 = (f32[2,40,256]{2,1,0:T(8,128)S(1)}, f32[2,40,256]{2,1,0:T(8,128)S(1)}, u32[]{:S(2)}, u32[]{:S(2)}) collective-permute-start(f32[2,40,256]{2,1,0:T(8,128)S(1)} %all_gather.3), channel_id=1, source_target_pairs={{0,2},{2,4},{4,6},{6,8},{8,10},{10,12},{12,14},{14,16},{16,18},{18... | collective-permute-start | bytes 245768 | tf_op jit(solution)/shard_map/ppermute | solution.py:22
  9.9 3.4 %collective-permute-start = (f32[2,40,256]{2,1,0:T(8,128)S(1)}, f32[2,40,256]{2,1,0:T(8,128)S(1)}, u32[]{:S(2)}, u32[]{:S(2)}) collective-permute-start(f32[2,40,256]{2,1,0:T(8,128)S(1)} %all_gather.3), channel_id=1, source_target_pairs={{0,4},{2,6},{4,8},{6,10},{8,12},{10,14},{12,16},{14,18},{16,20},{1... | collective-permute-start | bytes 245768 | tf_op jit(solution)/shard_map/ppermute | solution.py:22
  13.4 0.0 copy-start.3
  13.4 0.6 copy-done.3
  14.0 0.1 compare_convert_fusion.1
  14.1 0.0 copy-start.4
  14.1 0.1 compare_select_fusion.1
  14.2 0.6 copy-done.4
  14.8 0.1 add_bitcast_fusion.cond_ref
  14.8 0.1 add_bitcast_fusion.1.pred_ref
  14.9 0.0 collective-permute-done.1
  14.9 0.5 collective-permute-done
  15.4 0.0 copy-start.1
  15.4 0.0 copy-start
  15.4 0.0 copy-start.2
  15.4 0.6 copy-done.1
  16.1 0.0 copy-done
  16.1 0.0 copy-done.2
  16.1 47.8 %both.1 = (f32[32,256]{1,0:T(8,128)}, f32[8,128]{1,0:T(8,128)S(1)}, f32[32,256]{1,0:T(8,128)}) custom-call(f32[6,40,256]{2,1,0:T(8,128)S(1)} %pad_maximum_fusion.window_ref, f32[8,128]{1,0:T(8,128)S(1)} %bitcast.10, s32[8]{0:T(128)S(1)} %add_bitcast_fusion.cond_ref, s32[6]{0:T(128)S(1)} %add_bitcast_fusion.1.pred_ref, f32[2,256]{1,0:T(2,128)S(1)} %bitcast.11, ...), custom_call_target="tpu_custom_call" | custom-call | tf_op jit(solution)/shard_map/both/pallas_call | solution.py:384
  64.0 0.0 collective-permute-start.2
  64.0 1.1 %collective-permute-done.2 = f32[1,128]{1,0:T(1,128)S(1)} collective-permute-done((f32[1,128]{1,0:T(1,128)S(1)}, f32[1,128]{1,0:T(1,128)S(1)}, u32[]{:S(2)}, u32[]{:S(2)}) %collective-permute-start.2) | collective-permute-done | bytes 544 | tf_op jit(solution)/shard_map/ppermute | solution.py:35
  65.1 1.5 %collective-permute-start.3 = (f32[1,128]{1,0:T(1,128)S(1)}, f32[1,128]{1,0:T(1,128)S(1)}, u32[]{:S(2)}, u32[]{:S(2)}) collective-permute-start(f32[1,128]{1,0:T(1,128)S(1)} %slice_add_fusion), channel_id=1, source_target_pairs={{0,2},{2,0},{4,6},{6,4},{8,10},{10,8},{12,14},{14,12},{16,18},{18,... | collective-permute-start | bytes 1544 | tf_op jit(solution)/shard_map/ppermute | solution.py:35
  66.6 2.1 %collective-permute-done.3 = f32[1,128]{1,0:T(1,128)S(1)} collective-permute-done((f32[1,128]{1,0:T(1,128)S(1)}, f32[1,128]{1,0:T(1,128)S(1)}, u32[]{:S(2)}, u32[]{:S(2)}) %collective-permute-start.3) | collective-permute-done | bytes 544 | tf_op jit(solution)/shard_map/ppermute | solution.py:35
  68.6 2.4 %collective-permute-start.4 = (f32[1,128]{1,0:T(1,128)S(1)}, f32[1,128]{1,0:T(1,128)S(1)}, u32[]{:S(2)}, u32[]{:S(2)}) collective-permute-start(f32[1,128]{1,0:T(1,128)S(1)} %add.22), channel_id=1, source_target_pairs={{0,4},{2,6},{4,0},{6,2},{8,12},{10,14},{12,8},{14,10},{16,20},{18,... | collective-permute-start | bytes 1544 | tf_op jit(solution)/shard_map/ppermute | solution.py:35
  71.0 1.5 %collective-permute-done.4 = f32[1,128]{1,0:T(1,128)S(1)} collective-permute-done((f32[1,128]{1,0:T(1,128)S(1)}, f32[1,128]{1,0:T(1,128)S(1)}, u32[]{:S(2)}, u32[]{:S(2)}) %collective-permute-start.4) | collective-permute-done | bytes 544 | tf_op jit(solution)/shard_map/ppermute | solution.py:35
  72.5 3.0 %collective-permute-start.5 = (f32[1,128]{1,0:T(1,128)S(1)}, f32[1,128]{1,0:T(1,128)S(1)}, u32[]{:S(2)}, u32[]{:S(2)}) collective-permute-start(f32[1,128]{1,0:T(1,128)S(1)} %add.23), channel_id=1, source_target_pairs={{0,8},{2,10},{4,12},{6,14},{8,0},{10,2},{12,4},{14,6},{16,24},{18,... | collective-permute-start | bytes 1544 | tf_op jit(solution)/shard_map/ppermute | solution.py:35
  75.5 1.5 %collective-permute-done.5 = f32[1,128]{1,0:T(1,128)S(1)} collective-permute-done((f32[1,128]{1,0:T(1,128)S(1)}, f32[1,128]{1,0:T(1,128)S(1)}, u32[]{:S(2)}, u32[]{:S(2)}) %collective-permute-start.5) | collective-permute-done | bytes 544 | tf_op jit(solution)/shard_map/ppermute | solution.py:35
  77.0 3.0 %collective-permute-start.6 = (f32[1,128]{1,0:T(1,128)S(1)}, f32[1,128]{1,0:T(1,128)S(1)}, u32[]{:S(2)}, u32[]{:S(2)}) collective-permute-start(f32[1,128]{1,0:T(1,128)S(1)} %add.24), channel_id=1, source_target_pairs={{0,16},{2,18},{4,20},{6,22},{8,24},{10,26},{12,28},{14,30},{16,0},... | collective-permute-start | bytes 1544 | tf_op jit(solution)/shard_map/ppermute | solution.py:35
  80.1 1.5 %collective-permute-done.6 = f32[1,128]{1,0:T(1,128)S(1)} collective-permute-done((f32[1,128]{1,0:T(1,128)S(1)}, f32[1,128]{1,0:T(1,128)S(1)}, u32[]{:S(2)}, u32[]{:S(2)}) %collective-permute-start.6) | collective-permute-done | bytes 544 | tf_op jit(solution)/shard_map/ppermute | solution.py:35
  81.6 0.6 fusion
  (9 shorter events, 0.0 us)
Async XLA Ops:
  5.2 9.7 %collective-permute-start.1 = (f32[2,40,256]{2,1,0:T(8,128)S(1)}, f32[2,40,256]{2,1,0:T(8,128)S(1)}, u32[]{:S(2)}, u32[]{:S(2)}) collective-permute-start(f32[2,40,256]{2,1,0:T(8,128)S(1)} %all_gather.3), channel_id=1, source_target_pairs={{0,2},{2,4},{4,6},{6,8},{8,10},{10,12},{12,14},{14,16},{16,18},{18... | collective-permute-start | bytes 245768 | tf_op jit(solution)/shard_map/ppermute | solution.py:22
  9.9 5.5 %collective-permute-start = (f32[2,40,256]{2,1,0:T(8,128)S(1)}, f32[2,40,256]{2,1,0:T(8,128)S(1)}, u32[]{:S(2)}, u32[]{:S(2)}) collective-permute-start(f32[2,40,256]{2,1,0:T(8,128)S(1)} %all_gather.3), channel_id=1, source_target_pairs={{0,4},{2,6},{4,8},{6,10},{8,12},{10,14},{12,16},{14,18},{16,20},{1... | collective-permute-start | bytes 245768 | tf_op jit(solution)/shard_map/ppermute | solution.py:22
  13.4 0.7 copy-start.3
  14.1 0.7 copy-start.4
  15.4 0.7 copy-start.1
  15.4 0.7 copy-start
  15.4 0.7 copy-start.2
  64.0 1.1 %collective-permute-start.2 = (f32[1,128]{1,0:T(1,128)S(1)}, f32[1,128]{1,0:T(1,128)S(1)}, u32[]{:S(2)}, u32[]{:S(2)}) collective-permute-start(f32[1,128]{1,0:T(1,128)S(1)} %slice.9), channel_id=1, source_target_pairs={{0,1},{1,0},{2,3},{3,2},{4,5},{5,4},{6,7},{7,6},{8,9},{9,8},{10,11... | collective-permute-start | bytes 1544 | tf_op jit(solution)/shard_map/ppermute | solution.py:35
  65.1 3.5 %collective-permute-start.3 = (f32[1,128]{1,0:T(1,128)S(1)}, f32[1,128]{1,0:T(1,128)S(1)}, u32[]{:S(2)}, u32[]{:S(2)}) collective-permute-start(f32[1,128]{1,0:T(1,128)S(1)} %slice_add_fusion), channel_id=1, source_target_pairs={{0,2},{2,0},{4,6},{6,4},{8,10},{10,8},{12,14},{14,12},{16,18},{18,... | collective-permute-start | bytes 1544 | tf_op jit(solution)/shard_map/ppermute | solution.py:35
  68.6 3.9 %collective-permute-start.4 = (f32[1,128]{1,0:T(1,128)S(1)}, f32[1,128]{1,0:T(1,128)S(1)}, u32[]{:S(2)}, u32[]{:S(2)}) collective-permute-start(f32[1,128]{1,0:T(1,128)S(1)} %add.22), channel_id=1, source_target_pairs={{0,4},{2,6},{4,0},{6,2},{8,12},{10,14},{12,8},{14,10},{16,20},{18,... | collective-permute-start | bytes 1544 | tf_op jit(solution)/shard_map/ppermute | solution.py:35
  72.5 4.5 %collective-permute-start.5 = (f32[1,128]{1,0:T(1,128)S(1)}, f32[1,128]{1,0:T(1,128)S(1)}, u32[]{:S(2)}, u32[]{:S(2)}) collective-permute-start(f32[1,128]{1,0:T(1,128)S(1)} %add.23), channel_id=1, source_target_pairs={{0,8},{2,10},{4,12},{6,14},{8,0},{10,2},{12,4},{14,6},{16,24},{18,... | collective-permute-start | bytes 1544 | tf_op jit(solution)/shard_map/ppermute | solution.py:35
  77.0 4.5 %collective-permute-start.6 = (f32[1,128]{1,0:T(1,128)S(1)}, f32[1,128]{1,0:T(1,128)S(1)}, u32[]{:S(2)}, u32[]{:S(2)}) collective-permute-start(f32[1,128]{1,0:T(1,128)S(1)} %add.24), channel_id=1, source_target_pairs={{0,16},{2,18},{4,20},{6,22},{8,24},{10,26},{12,28},{14,30},{16,0},... | collective-permute-start | bytes 1544 | tf_op jit(solution)/shard_map/ppermute | solution.py:35

commit v3 on v2

--- a/solution.py
+++ b/solution.py
@@ -20,21 +20,6 @@
     count = lax.axis_size(axis)
     initial, last = (max(0, -steps), min(count, count - steps))
     return lax.ppermute(value, axis, [(source, source + steps) for source in range(initial, last)])
-
-
-def summed_over(value, axis):
-    count = lax.axis_size(axis)
-    if count & (count - 1):
-        total = value
-        for _ in range(count - 1):
-            value = lax.ppermute(value, axis, [(i, (i + 1) % count) for i in range(count)])
-            total = total + value
-        return total
-    step = 1
-    while step < count:
-        value = value + lax.ppermute(value, axis, [(i, i ^ step) for i in range(count)])
-        step *= 2
-    return value
 
 
 def prepare_kernel(values_ref, coords_ref, valid_ref, theta_ref, packed_ref, extra_ref):
@@ -99,11 +84,15 @@
 
     diag = [over_lanes(rows[lo], 8 * lo + j) for j in range(8)]
     extract(lo)
+    ahead = [over_lanes(rows[lo + 1], 8 * (lo + 1) + j) for j in range(8)]
     yield
     for p in range(lo, hi):
         panel = (lane >= 8 * p) & (lane < 8 * p + 8)
         start = jnp.where(panel, jnp.where(lane == sub + 8 * p, 1.0, 0.0), rows[p])
         solved, product, kept = start, None, []
+        near = p + 1 < hi
+        if near:
+            cols = [cols_ref[p % 2, (p + 1 - lo) * 8 + j] for j in range(8)]
         for j in range(0, 8, 2):
             x, y = diag[j], diag[j + 1]
             a, b, c = over_sublanes(x, j), over_sublanes(x, j + 1), over_sublanes(y, j + 1)
@@ -111,9 +100,17 @@
             recip = 1.0 / det
             x, y = x - unit[j], y - unit[j + 1]
             nx, ny = c * x - b * y, a * y - b * x
+            if near:
+                s, t = cols[j], cols[j + 1]
+                ns, nt = (c * s - b * t) * recip, (a * t - b * s) * recip
             for k in range(j + 2, 8):
                 u, v = over_sublanes(diag[k], j), over_sublanes(diag[k], j + 1)
                 diag[k] = diag[k] - (nx * u + ny * v) * recip
+                if near:
+                    cols[k] = cols[k] - (ns * u + nt * v)
+            if near:
+                for k in range(8):
+                    ahead[k] = ahead[k] - (ns * over_sublanes(s, k) + nt * over_sublanes(t, k))
             solved = solved - (nx * over_sublanes(solved, j) + ny * over_sublanes(solved, j + 1)) * recip
             kept.append((a, b, recip, nx, ny))
             product = det if product is None else product * det
@@ -126,11 +123,13 @@
                 rows[q] = jnp.where(panel, 0.0, rows[q]) - moved
 
             update(p + 1)
-            diag = [over_lanes(rows[p + 1], 8 * (p + 1) + j) for j in range(8)]
+            diag = ahead
             yield
             for q in range(p + 2, hi):
                 update(q)
             extract(p + 1)
+            if p + 2 < hi:
+                ahead = [over_lanes(rows[p + 2], 8 * (p + 2) + j) for j in range(8)]
         lower = start
         scale, fix = jnp.zeros(GROUP, jnp.float32), jnp.zeros(GROUP, jnp.float32)
         for j in range(0, 8, 2):
@@ -407,8 +406,9 @@
         whitened.append(white)
         terms.append(term)
         predicted.append(field)
-    total = sum(terms[1:], terms[0])[0:1]
-    total = summed_over(summed_over(total, "blk"), "space")
+    devices = lax.axis_size("space") * n_blk
+    total = jnp.broadcast_to(sum(terms[1:], terms[0])[0:1], (devices, 1, TILE))
+    total = jnp.sum(lax.all_to_all(total, ("space", "blk"), 0, 0, tiled=True), axis=0)
     loglik = total[0, 0] / (reps * total[0, 1])
     return jnp.stack(whitened), jnp.stack(predicted), loglik
 

time: 84.9 us -> 74.5 us (0.88)
  blocking collectives: 2.17 us -> 15.8 us
  starting transfers between devices: 18 us -> 8.16 us
  waiting for transfers between devices: 8.2 us -> 0.48 us
  Pallas kernels: 49.6 us -> 43.2 us
    all_to_all x0 -> x1, blocking collectives: none -> 13.6 us  [body(): lax.all_to_all(total, ('space', 'blk'), 0, 0, tiled=True)]
    ppermute x5 -> x0, starting transfers between devices: 9.88 us -> none  [summed_over(): lax.ppermute(value, axis, [(i, i ^ step) for i in range(count)])]
    ppermute x5 -> x0, waiting for transfers between devices: 7.72 us -> none  [summed_over(): lax.ppermute(value, axis, [(i, i ^ step) for i in range(count)])]
    pallas_call x1, Pallas kernels: 47.8 us -> 41.5 us  [body(): pl.pallas_call(functools.partial(both_kernel, reps=reps, sets=sets, sourc...]
  transfers between devices with their start and end apart: 7 -> 2, of which waited for: 6 -> 1; matrix products, arithmetic and copies ran while one was open for 0% -> 0% of each run, Pallas kernels for 0% -> 0%
where the time goes in v3:
time: 74.5 us; the launch traced here: 74.2 us
  Pallas kernels  43.2 us (58%)
  blocking collectives  15.8 us (21%)
  starting transfers between devices  8.16 us (11%)
  between operations  3.68 us (5%)
  local copies, waits for them, and re-layouts  2.51 us (3%)
    pallas_call x1, Pallas kernels, body(): pl.pallas_call(functools.partial(both_kernel, reps=reps, sets=sets, sourc...  41.5 us
    all_to_all x1, blocking collectives, body(): lax.all_to_all(total, ('space', 'blk'), 0, 0, tiled=True)  13.6 us
    ppermute x2, starting transfers between devices, passed_along(): lax.ppermute(value, axis, [(source, source + steps) for source in range(i...  8.16 us
    all_gather x1, blocking collectives, body(): grouped = lax.all_gather(packed, 'blk', axis=0, tiled=True)  2.17 us
    unnamed x10, local copies, waits for them, and re-layouts  1.91 us
    pallas_call x1, Pallas kernels, body(): pl.pallas_call(prepare_kernel, out_shape=(jax.ShapeDtypeStruct((blocks, R...  1.74 us
  transfers between devices with their start and end apart: 2, of which 1 were waited for; matrix products, arithmetic and copies ran while one was open for 0% of the time, Pallas kernels for 0%

profile of v3, /device:TPU:0, one launch (start us, length us, event | category | flops | bytes accessed | tf_op | source)
XLA Modules:
  0.0 74.2 jit_solution(6412833031913623171)
XLA Ops:
  1.3 1.7 %prepare.1 = (f32[1,40,256]{2,1,0:T(8,128)}, f32[1,8,128]{2,1,0:T(8,128)}) custom-call(f32[1,32,256]{2,1,0:T(8,128)} %values_ref.1, f32[1,2,256]{2,1,0:T(2,128)} %coords_ref.1, s32[1]{0:T(128)S(6)} %copy.11.valid_ref, f32[6]{0:T(128)} %theta_ref.3), custom_call_target="tpu_custom_call" | custom-call | tf_op jit(solution)/shard_map/prepare/pallas_call | solution.py:354
  3.0 2.2 %all_gather.3 = f32[2,40,256]{2,1,0:T(8,128)S(1)} all-gather(f32[1,40,256]{2,1,0:T(8,128)} %get-tuple-element.8), channel_id=1, replica_groups=mesh['space'=16,'blk'=2] {'blk'}, dimensions={0}, use_global_device_ids=true | all-gather | bytes 122880 | tf_op jit(solution)/shard_map/all_gather | solution.py:364
  5.2 4.7 %collective-permute-start.1 = (f32[2,40,256]{2,1,0:T(8,128)S(1)}, f32[2,40,256]{2,1,0:T(8,128)S(1)}, u32[]{:S(2)}, u32[]{:S(2)}) collective-permute-start(f32[2,40,256]{2,1,0:T(8,128)S(1)} %all_gather.3), channel_id=1, source_target_pairs={{0,2},{2,4},{4,6},{6,8},{8,10},{10,12},{12,14},{14,16},{16,18},{18... | collective-permute-start | bytes 245768 | tf_op jit(solution)/shard_map/ppermute | solution.py:22
  9.9 3.4 %collective-permute-start = (f32[2,40,256]{2,1,0:T(8,128)S(1)}, f32[2,40,256]{2,1,0:T(8,128)S(1)}, u32[]{:S(2)}, u32[]{:S(2)}) collective-permute-start(f32[2,40,256]{2,1,0:T(8,128)S(1)} %all_gather.3), channel_id=1, source_target_pairs={{0,4},{2,6},{4,8},{6,10},{8,12},{10,14},{12,16},{14,18},{16,20},{1... | collective-permute-start | bytes 245768 | tf_op jit(solution)/shard_map/ppermute | solution.py:22
  13.4 0.0 copy-start.3
  13.4 0.6 copy-done.3
  14.0 0.1 compare_convert_fusion.1
  14.1 0.0 copy-start.4
  14.1 0.1 compare_select_fusion.1
  14.2 0.6 copy-done.4
  14.8 0.1 add_bitcast_fusion.cond_ref
  14.8 0.1 add_bitcast_fusion.1.pred_ref
  14.9 0.0 collective-permute-done.1
  14.9 0.5 collective-permute-done
  15.4 0.0 copy-start.1
  15.4 0.0 copy-start
  15.4 0.0 copy-start.2
  15.4 0.6 copy-done.1
  16.1 0.0 copy-done
  16.1 0.0 copy-done.2
  16.1 41.5 %both.1 = (f32[32,256]{1,0:T(8,128)}, f32[8,128]{1,0:T(8,128)S(1)}, f32[32,256]{1,0:T(8,128)}) custom-call(f32[6,40,256]{2,1,0:T(8,128)S(1)} %pad_maximum_fusion.window_ref, f32[8,128]{1,0:T(8,128)S(1)} %bitcast.14, s32[8]{0:T(128)S(1)} %add_bitcast_fusion.cond_ref, s32[6]{0:T(128)S(1)} %add_bitcast_fusion.1.pred_ref, f32[2,256]{1,0:T(2,128)S(1)} %bitcast.15, ...), custom_call_target="tpu_custom_call" | custom-call | tf_op jit(solution)/shard_map/both/pallas_call | solution.py:383
  57.6 13.6 %all_to_all.5 = f32[32,1,128]{2,1,0:T(1,128)S(1)} all-to-all(f32[32,1,128]{2,1,0:T(1,128)S(1)} %broadcast_in_dim.7), channel_id=1, replica_groups=mesh['space'=16,'blk'=2] {'space','blk'}, dimensions={0} | all-to-all | bytes 32768 | tf_op jit(solution)/shard_map/all_to_all | solution.py:411
  71.3 0.6 fusion
  (6 shorter events, 0.1 us)
Async XLA Ops:
  5.2 9.7 %collective-permute-start.1 = (f32[2,40,256]{2,1,0:T(8,128)S(1)}, f32[2,40,256]{2,1,0:T(8,128)S(1)}, u32[]{:S(2)}, u32[]{:S(2)}) collective-permute-start(f32[2,40,256]{2,1,0:T(8,128)S(1)} %all_gather.3), channel_id=1, source_target_pairs={{0,2},{2,4},{4,6},{6,8},{8,10},{10,12},{12,14},{14,16},{16,18},{18... | collective-permute-start | bytes 245768 | tf_op jit(solution)/shard_map/ppermute | solution.py:22
  9.9 5.5 %collective-permute-start = (f32[2,40,256]{2,1,0:T(8,128)S(1)}, f32[2,40,256]{2,1,0:T(8,128)S(1)}, u32[]{:S(2)}, u32[]{:S(2)}) collective-permute-start(f32[2,40,256]{2,1,0:T(8,128)S(1)} %all_gather.3), channel_id=1, source_target_pairs={{0,4},{2,6},{4,8},{6,10},{8,12},{10,14},{12,16},{14,18},{16,20},{1... | collective-permute-start | bytes 245768 | tf_op jit(solution)/shard_map/ppermute | solution.py:22
  13.4 0.7 copy-start.3
  14.1 0.7 copy-start.4
  15.4 0.7 copy-start.1
  15.4 0.7 copy-start
  15.4 0.7 copy-start.2

commit v4 on v3

--- a/solution.py
+++ b/solution.py
@@ -169,17 +169,15 @@
     logs_ref[...] = tree_sum(logs)
 
 
-def take_turns(streams, lead):
-    for i, stream in enumerate(streams):
-        for _ in range(lead * (len(streams) - 1 - i)):
-            next(stream, None)
-    live = list(streams)
+def take_turns(streams):
+    live = [[0.0, i, stream, weight] for i, (stream, weight) in enumerate(streams)]
     while live:
-        for stream in list(live):
-            try:
-                next(stream)
-            except StopIteration:
-                live.remove(stream)
+        entry = min(live)
+        try:
+            next(entry[2])
+            entry[0] += 1.0 / entry[3]
+        except StopIteration:
+            live.remove(entry)
 
 
 def decay(dx, dy, slope):
@@ -243,46 +241,67 @@
     return lax.dot(left, right, preferred_element_type=jnp.float32)
 
 
-def eliminate(systems, lo, hi, cols_ref, li_ref):
-    def step(k, carry):
-        off = pl.multiple_of(k * TILE, TILE)
-        streams = []
-        for i, (w_ref, logs_ref, _, _) in enumerate(systems):
-            rows = [w_ref[pl.ds(off + 8 * q, 8), pl.ds(off, TILE)] for q in range(TILE // 8)]
-            streams.append(factor_tile(rows, cols_ref.at[i], li_ref.at[i], logs_ref.at[k]))
-        take_turns(streams, 3)
-        for kk in range(lo, hi):
-
-            @pl.when(k == kk)
-            def _():
-                at = slice(kk * TILE, (kk + 1) * TILE)
-                start = (kk + 1) * TILE
-                rights, lefts = [], []
-                for i, (w_ref, _, tiles, total) in enumerate(systems):
-                    solved = product(left_parts(li_ref[i]), right_parts(w_ref[at, start:total]))
-                    w_ref[at, start:total] = solved
-                    if kk + 1 < tiles:
-                        rights.append(right_parts(solved))
-                        lefts.append(left_parts(jnp.transpose(solved[:, : tiles * TILE - start])))
-                row = kk + 1
-                while row < max(system[2] for system in systems):
-                    end = row + 2 - row % 2
-                    for i, (w_ref, _, tiles, total) in enumerate(systems):
-                        if row < tiles:
-                            first, last = row * TILE, end * TILE
-                            w_ref[first:last, first:total] -= product(
-                                lefts[i][first - start : last - start], rights[i][:, first - start :]
-                            )
-                    row = end
-
-        return carry
-
-    lax.fori_loop(lo, hi, step, 0)
+def eliminate(w_ref, logs_ref, tiles, total, cols_ref, li_ref, left_ref, right_ref):
+    sites = tiles * TILE
+
+    def rest(k, inverse, turned):
+        at, first = slice(k * TILE, (k + 1) * TILE), (k + 2) * TILE
+        chunks, lo = [], first
+        while lo < total:
+            hi = min(lo + 2 * TILE - lo % (2 * TILE) if lo < sites else lo + 2 * TILE, total)
+            if lo < sites:
+                hi = min(hi, sites)
+            chunks.append(slice(lo, hi))
+            lo = hi
+        below = slice((k + 1) * TILE, first)
+        for chunk in chunks:
+            solved = product(inverse, right_parts(w_ref[at, chunk]))
+            w_ref[at, chunk] = solved
+            if k + 1 < tiles:
+                right_ref[:, chunk] = right_parts(solved)
+                yield
+                w_ref[below, chunk] -= product(turned, right_ref[:, chunk])
+                if chunk.start < sites:
+                    left_ref[chunk, :] = left_parts(jnp.transpose(solved))
+            yield
+        for i, rows_at in enumerate(chunks):
+            if rows_at.start < sites:
+                for chunk in chunks[i:]:
+                    w_ref[rows_at, chunk] -= product(left_ref[rows_at, :], right_ref[:, chunk])
+                    yield
+
+    pending = iter(())
+    for k in range(tiles):
+        at = slice(k * TILE, (k + 1) * TILE)
+        rows = [w_ref[k * TILE + 8 * q : k * TILE + 8 * q + 8, at] for q in range(TILE // 8)]
+        beats = 0
+        for _ in factor_tile(rows, cols_ref, li_ref, logs_ref.at[k]):
+            beats += 1
+            if beats % 3 == 0:
+                next(pending, None)
+            yield
+        for _ in pending:
+            yield
+        inverse = left_parts(li_ref[...])
+        turned = None
+        if k + 1 < tiles:
+            near = slice((k + 1) * TILE, (k + 2) * TILE)
+            solved = product(inverse, right_parts(w_ref[at, near]))
+            w_ref[at, near] = solved
+            yield
+            turned = left_parts(jnp.transpose(solved))
+            w_ref[near, near] -= product(turned, right_parts(solved))
+            yield
+            pending = rest(k, inverse, turned)
+        else:
+            start = (k + 1) * TILE
+            w_ref[at, start:total] = product(inverse, right_parts(w_ref[at, start:total]))
 
 
 def both_kernel(
     window_ref, extra_ref, cond_ref, pred_ref, grid_ref, theta_ref, white_ref, term_ref, out_ref,
-    wc_ref, wp_ref, xb_ref, yb_ref, mb_ref, cols_ref, li_ref, lc_ref, lp_ref, *, reps, sets, sources,
+    wc_ref, wp_ref, xb_ref, yb_ref, mb_ref, cols_ref, li_ref, lc_ref, lp_ref,
+    left_c_ref, left_p_ref, right_c_ref, right_p_ref, *, reps, sets, sources,
 ):
     width, points = window_ref.shape[2], grid_ref.shape[1]
 
@@ -307,11 +326,12 @@
     count, data_at = sets * width // TILE, sets * width
     load_set(listed(cond_ref, sets), window_ref, theta_ref, reps, width, wc_ref, xb_ref, yb_ref, mb_ref, data_at)
     conditioning = (wc_ref, lc_ref, count, data_at + TILE)
-    both = min(predicting[2], count)
-    eliminate([conditioning, predicting], 0, both, cols_ref, li_ref)
-    for system in (conditioning, predicting):
-        if system[2] > both:
-            eliminate([system], both, system[2], cols_ref, li_ref)
+    take_turns(
+        [
+            (eliminate(*conditioning, cols_ref.at[0], li_ref.at[0], left_c_ref, right_c_ref), conditioning[2]),
+            (eliminate(*predicting, cols_ref.at[1], li_ref.at[1], left_p_ref, right_p_ref), predicting[2]),
+        ]
+    )
 
     own = slice((sets - 1) * width, sets * width)
     white = jnp.transpose(wc_ref[own, data_at : data_at + TILE])[0:reps, :]
@@ -399,6 +419,10 @@
                 pltpu.VMEM((2, TILE, TILE), jnp.float32),
                 pltpu.VMEM((sites // TILE,) + GROUP, jnp.float32),
                 pltpu.VMEM((near // TILE,) + GROUP, jnp.float32),
+                pltpu.VMEM((sites, 6 * TILE), jnp.bfloat16),
+                pltpu.VMEM((near, 6 * TILE), jnp.bfloat16),
+                pltpu.VMEM((6 * TILE, sites + TILE), jnp.bfloat16),
+                pltpu.VMEM((6 * TILE, near + TILE + points), jnp.bfloat16),
             ],
             compiler_params=PARAMS,
             name="both",

time: 74.5 us -> 69.1 us (0.928)
  Pallas kernels: 43.2 us -> 37.8 us
    pallas_call x1, Pallas kernels: 41.5 us -> 36.1 us  [body(): pl.pallas_call(functools.partial(both_kernel, reps=reps, sets=sets, sourc...]
where the time goes in v4:
time: 69.1 us; the launch traced here: 68.7 us
  Pallas kernels  37.8 us (55%)
  blocking collectives  15.8 us (23%)
  starting transfers between devices  8.16 us (12%)
  between operations  3.68 us (5%)
  local copies, waits for them, and re-layouts  2.51 us (4%)
    pallas_call x1, Pallas kernels, body(): pl.pallas_call(functools.partial(both_kernel, reps=reps, sets=sets, sourc...  36.1 us
    all_to_all x1, blocking collectives, body(): lax.all_to_all(total, ('space', 'blk'), 0, 0, tiled=True)  13.6 us
    ppermute x2, starting transfers between devices, passed_along(): lax.ppermute(value, axis, [(source, source + steps) for source in range(i...  8.16 us
    all_gather x1, blocking collectives, body(): grouped = lax.all_gather(packed, 'blk', axis=0, tiled=True)  2.17 us
    unnamed x10, local copies, waits for them, and re-layouts  1.91 us
    pallas_call x1, Pallas kernels, body(): pl.pallas_call(prepare_kernel, out_shape=(jax.ShapeDtypeStruct((blocks, R...  1.74 us
  transfers between devices with their start and end apart: 2, of which 1 were waited for; matrix products, arithmetic and copies ran while one was open for 0% of the time, Pallas kernels for 0%

profile of v4, /device:TPU:0, one launch (start us, length us, event | category | flops | bytes accessed | tf_op | source)
XLA Modules:
  0.0 68.7 jit_solution(2372478180614528995)
XLA Ops:
  1.3 1.7 %prepare.1 = (f32[1,40,256]{2,1,0:T(8,128)}, f32[1,8,128]{2,1,0:T(8,128)}) custom-call(f32[1,32,256]{2,1,0:T(8,128)} %values_ref.1, f32[1,2,256]{2,1,0:T(2,128)} %coords_ref.1, s32[1]{0:T(128)S(6)} %copy.11.valid_ref, f32[6]{0:T(128)} %theta_ref.3), custom_call_target="tpu_custom_call" | custom-call | tf_op jit(solution)/shard_map/prepare/pallas_call | solution.py:374
  3.0 2.2 %all_gather.3 = f32[2,40,256]{2,1,0:T(8,128)S(1)} all-gather(f32[1,40,256]{2,1,0:T(8,128)} %get-tuple-element.8), channel_id=1, replica_groups=mesh['space'=16,'blk'=2] {'blk'}, dimensions={0}, use_global_device_ids=true | all-gather | bytes 122880 | tf_op jit(solution)/shard_map/all_gather | solution.py:384
  5.2 4.7 %collective-permute-start.1 = (f32[2,40,256]{2,1,0:T(8,128)S(1)}, f32[2,40,256]{2,1,0:T(8,128)S(1)}, u32[]{:S(2)}, u32[]{:S(2)}) collective-permute-start(f32[2,40,256]{2,1,0:T(8,128)S(1)} %all_gather.3), channel_id=1, source_target_pairs={{0,2},{2,4},{4,6},{6,8},{8,10},{10,12},{12,14},{14,16},{16,18},{18... | collective-permute-start | bytes 245768 | tf_op jit(solution)/shard_map/ppermute | solution.py:22
  9.9 3.4 %collective-permute-start = (f32[2,40,256]{2,1,0:T(8,128)S(1)}, f32[2,40,256]{2,1,0:T(8,128)S(1)}, u32[]{:S(2)}, u32[]{:S(2)}) collective-permute-start(f32[2,40,256]{2,1,0:T(8,128)S(1)} %all_gather.3), channel_id=1, source_target_pairs={{0,4},{2,6},{4,8},{6,10},{8,12},{10,14},{12,16},{14,18},{16,20},{1... | collective-permute-start | bytes 245768 | tf_op jit(solution)/shard_map/ppermute | solution.py:22
  13.4 0.0 copy-start.3
  13.4 0.6 copy-done.3
  14.0 0.1 compare_convert_fusion.1
  14.1 0.0 copy-start.4
  14.1 0.1 compare_select_fusion.1
  14.2 0.6 copy-done.4
  14.8 0.1 add_bitcast_fusion.cond_ref
  14.8 0.1 add_bitcast_fusion.1.pred_ref
  14.9 0.0 collective-permute-done.1
  14.9 0.5 collective-permute-done
  15.4 0.0 copy-start.1
  15.4 0.0 copy-start
  15.4 0.0 copy-start.2
  15.4 0.6 copy-done.1
  16.1 0.0 copy-done
  16.1 0.0 copy-done.2
  16.1 36.1 %both.1 = (f32[32,256]{1,0:T(8,128)}, f32[8,128]{1,0:T(8,128)S(1)}, f32[32,256]{1,0:T(8,128)}) custom-call(f32[6,40,256]{2,1,0:T(8,128)S(1)} %pad_maximum_fusion.window_ref, f32[8,128]{1,0:T(8,128)S(1)} %bitcast.14, s32[8]{0:T(128)S(1)} %add_bitcast_fusion.cond_ref, s32[6]{0:T(128)S(1)} %add_bitcast_fusion.1.pred_ref, f32[2,256]{1,0:T(2,128)S(1)} %bitcast.15, ...), custom_call_target="tpu_custom_call" | custom-call | tf_op jit(solution)/shard_map/both/pallas_call | solution.py:403
  52.2 13.6 %all_to_all.5 = f32[32,1,128]{2,1,0:T(1,128)S(1)} all-to-all(f32[32,1,128]{2,1,0:T(1,128)S(1)} %broadcast_in_dim.7), channel_id=1, replica_groups=mesh['space'=16,'blk'=2] {'space','blk'}, dimensions={0} | all-to-all | bytes 32768 | tf_op jit(solution)/shard_map/all_to_all | solution.py:435
  65.8 0.6 fusion
  (6 shorter events, 0.1 us)
Async XLA Ops:
  5.2 9.7 %collective-permute-start.1 = (f32[2,40,256]{2,1,0:T(8,128)S(1)}, f32[2,40,256]{2,1,0:T(8,128)S(1)}, u32[]{:S(2)}, u32[]{:S(2)}) collective-permute-start(f32[2,40,256]{2,1,0:T(8,128)S(1)} %all_gather.3), channel_id=1, source_target_pairs={{0,2},{2,4},{4,6},{6,8},{8,10},{10,12},{12,14},{14,16},{16,18},{18... | collective-permute-start | bytes 245768 | tf_op jit(solution)/shard_map/ppermute | solution.py:22
  9.9 5.5 %collective-permute-start = (f32[2,40,256]{2,1,0:T(8,128)S(1)}, f32[2,40,256]{2,1,0:T(8,128)S(1)}, u32[]{:S(2)}, u32[]{:S(2)}) collective-permute-start(f32[2,40,256]{2,1,0:T(8,128)S(1)} %all_gather.3), channel_id=1, source_target_pairs={{0,4},{2,6},{4,8},{6,10},{8,12},{10,14},{12,16},{14,18},{16,20},{1... | collective-permute-start | bytes 245768 | tf_op jit(solution)/shard_map/ppermute | solution.py:22
  13.4 0.7 copy-start.3
  14.1 0.7 copy-start.4
  15.4 0.7 copy-start.1
  15.4 0.7 %copy-start = (f32[1,8,128]{2,1,0:T(8,128)S(1)}, f32[1,8,128]{2,1,0:T(8,128)}, u32[]{:S(2)}) copy-start(f32[1,8,128]{2,1,0:T(8,128)} %get-tuple-element.9) | copy-start | bytes 12292
  15.4 0.7 copy-start.2
